TPU v7x, 32 devices: a whole 2x2x4 slice. The times are simulated.
32 devices in a mesh: dp: 4 (over y, core), fsdp: 8 (over z, x).
Axes of the slice: x: 2, y: 2, z: 4, core: 2. Of those that a mesh axis runs over, the one named last changes fastest.
Arguments:
- tokens: bfloat16 [16384, 1024], P(('dp', 'fsdp')), may hold values from -6 to 6
- cotangent: bfloat16 [16384, 1024], P(('dp', 'fsdp'))
- page_lengths: int32 [2, 32], P(None, ('dp', 'fsdp')), may hold values from 0 to 512, as said below
- layout_pos: int32 [2, 16384], P(None, ('dp', 'fsdp')), may hold values from 0 to 63
- attn_master: float32 [4, 1024, 1024], P(None, ('dp', 'fsdp'))
- attn_first: float32 [4, 1024, 1024], P(None, ('dp', 'fsdp'))
- attn_second: float32 [4, 1024, 1024], P(None, ('dp', 'fsdp')), as said below
- ffin_master: float32 [2, 1024, 2816], P(None, ('dp', 'fsdp')), may hold values from -0.1875 to 0.1875
- ffin_first: float32 [2, 1024, 2816], P(None, ('dp', 'fsdp'))
- ffin_second: float32 [2, 1024, 2816], P(None, ('dp', 'fsdp')), as said below
- down_master: float32 [1024, 2816], P(('dp', 'fsdp')), may hold values from -0.109375 to 0.109375
- down_first: float32 [1024, 2816], P(('dp', 'fsdp'))
- down_second: float32 [1024, 2816], P(('dp', 'fsdp')), as said below
- small_master: float32 [3584], P(('dp', 'fsdp'))
- small_first: float32 [3584], P(('dp', 'fsdp'))
- small_second: float32 [3584], P(('dp', 'fsdp')), as said below
Outputs:
- block_out: bfloat16 [16384, 1024], P(('dp', 'fsdp'))
- grad_tokens: float32 [16384, 1024], P(('dp', 'fsdp'))
- grad_norm: float32 [], replicated
- attn_master_new: float32 [4, 1024, 1024], P(None, ('dp', 'fsdp'))
- attn_first_new: float32 [4, 1024, 1024], P(None, ('dp', 'fsdp'))
- attn_second_new: float32 [3, 1024, 1024], P(None, ('dp', 'fsdp'))
- query_second_new: float32 [1024, 1024], P(('dp', 'fsdp'))
- ffin_master_new: float32 [2, 1024, 2816], P(None, ('dp', 'fsdp'))
- ffin_first_new: float32 [2, 1024, 2816], P(None, ('dp', 'fsdp'))
- ffin_second_new: float32 [2, 1024, 2816], P(None, ('dp', 'fsdp'))
- down_master_new: float32 [1024, 2816], P(('dp', 'fsdp'))
- down_first_new: float32 [1024, 2816], P(('dp', 'fsdp'))
- down_second_new: float32 [1024, 2816], P(('dp', 'fsdp'))
- small_master_new: float32 [3584], P(('dp', 'fsdp'))
- small_first_new: float32 [3584], P(('dp', 'fsdp'))
- small_second_new: float32 [3584], P(('dp', 'fsdp'))
Inputs may be any that keep to these rules, and one draw needn't show every extreme that they name: `page_lengths`: row 0 holds the length of a device's first page, 246 to 512 tokens; row 1 that of a second page packed right after it, or 0; a device's pages together hold at most 512 tokens, and some device holds a single page of 512 tokens. `attn_second`: Positive. `ffin_second`: Positive. `down_second`: Positive. `small_second`: Positive.
All inputs are finite; a program needn't handle non-finite values.
Results may differ from a plain program's by a relative error of at most 0.012.
The roundings to bfloat16 on the way count: a program that leaves them out, or rounds other values in their place, can miss the bound.
Values may be sent and summed in bfloat16 or wider, within the bound.
A program may use at most 256 MiB of HBM per device.

v0:
```python
import jax
import jax.numpy as jnp
import numpy as np
from jax import lax
from jax.sharding import PartitionSpec as P

HEADS = 16
HEAD_DIM = 64
BUCKETS = 32
LAYOUT_POS = 64
STEP = 10


norm_eps = 1e-06
adam_eps = 1e-08
beta_one = 0.5
beta_two = 0.5
clip_max = 1.0
matrix_rate = 0.02
small_rate = 0.4
decay_rate = 0.01
far_negative = -1e30
max_distance = 128
block_rows = 512


def relative_buckets(tok_count, buckets):
    offsets = np.arange(tok_count)[None, :] - np.arange(tok_count)[:, None]
    half_count = buckets // 2
    exact_count = half_count // 2
    distance = np.abs(offsets)
    far_bucket = exact_count + (
        np.log(np.maximum(distance, 1) / exact_count)
        / np.log(max_distance / exact_count)
        * (half_count - exact_count)
    ).astype(np.int64)
    far_bucket = np.minimum(far_bucket, half_count - 1)
    bucket_ids = (offsets > 0).astype(np.int64) * half_count + np.where(
        distance < exact_count, distance, far_bucket
    )
    return bucket_ids.astype(np.int32)


def layout_table(positions, buckets):
    offsets = np.arange(positions)[None, :] - np.arange(positions)[:, None]
    half_count = buckets // 2
    bucket_ids = np.clip(offsets, -half_count, half_count - 1) + half_count
    return (np.arange(buckets)[:, None] == bucket_ids.reshape(1, -1)).astype(np.float32)


def scaled_norm(values, gain):
    return values * lax.rsqrt(jnp.mean(values * values, axis=-1, keepdims=True) + norm_eps) * gain


def gated_gelu(gate_pre, up_pre):
    return jax.nn.gelu(gate_pre, approximate=True) * up_pre


def adamw_update(master, first_state, second_state, gradient, step_rate, weight_decay):
    first_new = beta_one * first_state + (1.0 - beta_one) * gradient
    second_new = beta_two * second_state + (1.0 - beta_two) * gradient * gradient
    first_hat = first_new / (1.0 - beta_one**STEP)
    second_hat = second_new / (1.0 - beta_two**STEP)
    master_new = master - step_rate * (
        first_hat / (jnp.sqrt(second_hat) + adam_eps) + weight_decay * master
    )
    return (master_new, first_new, second_new)


def on_device(
    tokens,
    cotangent,
    page_lengths,
    layout_pos,
    attn_master,
    attn_first,
    attn_second,
    ffin_master,
    ffin_first,
    ffin_second,
    down_master,
    down_first,
    down_second,
    small_master,
    small_first,
    small_second,
):
    f32 = jnp.float32
    bf16 = jnp.bfloat16
    highest = lax.Precision.HIGHEST
    tok_count, model_width = tokens.shape
    attn_low = attn_master.astype(bf16)
    ffin_low = ffin_master.astype(bf16)
    down_low = down_master.astype(bf16)
    small_low = small_master.astype(bf16)
    w_attn, w_in, w_down, small_all = (
        lax.all_gather(attn_low, ("dp", "fsdp"), axis=1, tiled=True),
        lax.all_gather(ffin_low, ("dp", "fsdp"), axis=1, tiled=True),
        lax.all_gather(down_low, ("dp", "fsdp"), axis=0, tiled=True),
        lax.all_gather(small_low, ("dp", "fsdp"), axis=0, tiled=True),
    )
    gain_one = small_all[:model_width].astype(f32)
    gain_two = small_all[model_width : 2 * model_width].astype(f32)
    tables_t = jnp.transpose(small_all[2 * model_width :].reshape(3, BUCKETS, HEADS), (0, 2, 1))
    layout_hot = jnp.asarray(layout_table(LAYOUT_POS, BUCKETS))
    kernels = jnp.einsum(
        "khn,nm->khm", tables_t[1:], layout_hot.astype(bf16), preferred_element_type=f32
    )
    kernels = kernels.reshape(2, HEADS, LAYOUT_POS, LAYOUT_POS).astype(bf16)
    first_len = page_lengths[0, 0]
    both_len = page_lengths[0, 0] + page_lengths[1, 0]
    tok_index = jnp.arange(tok_count)
    page_ids = jnp.where(tok_index < first_len, 0, jnp.where(tok_index < both_len, 1, 2))
    valid_mask = tok_index < both_len
    valid_rows = valid_mask.astype(f32)[:, None]
    pos_grid = jnp.arange(LAYOUT_POS)
    pos_hot = (layout_pos[:, :, None] == pos_grid[None, None, :]).astype(bf16)
    pos_hot_f32 = pos_hot.astype(f32)
    rel_rows = jnp.asarray(relative_buckets(tok_count, BUCKETS))
    bucket_grid = jnp.arange(BUCKETS)
    rows_per_block = min(tok_count, block_rows)
    block_count = tok_count // rows_per_block
    block_starts = jnp.arange(block_count) * rows_per_block
    stream = tokens.astype(f32)
    normed_one = scaled_norm(stream, gain_one).astype(bf16)
    projected = jnp.einsum(
        "td,kde->kte", normed_one, w_attn[:3], preferred_element_type=f32
    ).astype(bf16)
    shaped = projected.reshape(3, tok_count, HEADS, HEAD_DIM)
    queries = shaped[0]
    key_rows = shaped[1]
    values = shaped[2]

    def block_scores(block_start, query_rows):
        rel_idx = lax.dynamic_slice_in_dim(rel_rows, block_start, rows_per_block, 0)
        rel_hot = (bucket_grid[:, None] == rel_idx.reshape(1, -1)).astype(bf16)
        bias_all = jnp.dot(tables_t[0], rel_hot, preferred_element_type=f32).reshape(
            HEADS, rows_per_block, tok_count
        )
        layout_rows = jnp.einsum(
            "kia,khab->khib", pos_hot, kernels, preferred_element_type=f32
        ).astype(bf16)
        bias_all = bias_all + jnp.einsum(
            "khib,kjb->hij", layout_rows, pos_hot, preferred_element_type=f32
        )
        scores = (
            jnp.einsum("ihe,jhe->hij", query_rows, key_rows, preferred_element_type=f32) + bias_all
        )
        allowed = (page_ids[:, None] == page_ids[None, :]) & valid_mask[None, :]
        masked = jnp.where(allowed[None], scores, far_negative)
        return (masked, allowed, rel_hot, pos_hot)

    def forward_block(running, block_start):
        masked, allowed, rel_hot, query_hot = block_scores(block_start, queries)
        row_max = jnp.max(masked, axis=-1, keepdims=True)
        exponent = jnp.exp(masked - row_max)
        row_total = jnp.sum(exponent, axis=-1, keepdims=True)
        weights_low = (exponent / row_total).astype(bf16)
        block_context = jnp.einsum("hij,jhe->ihe", weights_low, values, preferred_element_type=f32)
        return (running, (block_context, row_max + jnp.log(row_total)))

    unused_carry, (context_blocks, lse_blocks) = lax.scan(
        forward_block, jnp.zeros((), f32), block_starts
    )
    context = context_blocks.reshape(tok_count, model_width).astype(bf16)
    attended = jnp.dot(context, w_attn[3], preferred_element_type=f32)
    residual = stream + attended
    normed_two = scaled_norm(residual, gain_two).astype(bf16)
    gate_up = jnp.einsum("td,kdf->ktf", normed_two, w_in, preferred_element_type=f32)
    hidden = gated_gelu(gate_up[0], gate_up[1]).astype(bf16)
    mixed = jnp.einsum("tf,df->td", hidden, w_down, preferred_element_type=f32)
    block_out = (valid_rows * (residual + mixed)).astype(bf16)
    w_attn, w_in, w_down = (
        lax.all_gather(attn_low, ("dp", "fsdp"), axis=1, tiled=True),
        lax.all_gather(ffin_low, ("dp", "fsdp"), axis=1, tiled=True),
        lax.all_gather(down_low, ("dp", "fsdp"), axis=0, tiled=True),
    )
    grad_out = valid_rows * cotangent.astype(f32)
    grad_out_low = grad_out.astype(bf16)
    grad_down = jnp.einsum("td,tf->df", grad_out_low, hidden, preferred_element_type=f32)
    grad_hidden = jnp.einsum("td,df->tf", grad_out_low, w_down, preferred_element_type=f32)
    unused_gated, gated_pull = jax.vjp(gated_gelu, gate_up[0], gate_up[1])
    grad_gate, grad_up = gated_pull(grad_hidden)
    grad_gate_up = jnp.stack([grad_gate, grad_up]).astype(bf16)
    grad_in = jnp.einsum("td,ktf->kdf", normed_two, grad_gate_up, preferred_element_type=f32)
    grad_normed_two = jnp.einsum("ktf,kdf->td", grad_gate_up, w_in, preferred_element_type=f32)
    unused_second, norm_pull_two = jax.vjp(scaled_norm, residual, gain_two)
    grad_residual_norm, grad_gain_two = norm_pull_two(grad_normed_two)
    grad_residual = grad_out + grad_residual_norm
    grad_attended = grad_residual.astype(bf16)
    grad_out_proj = jnp.einsum("td,te->de", context, grad_attended, preferred_element_type=f32)
    grad_context = jnp.einsum(
        "te,de->td", grad_attended, w_attn[3], preferred_element_type=f32
    ).astype(bf16)
    grad_context = grad_context.reshape(tok_count, HEADS, HEAD_DIM)

    def backward_block(running, block_item):
        grad_key_rows, grad_value_rows, grad_rel, grad_layout = running
        block_start, lse_rows = block_item
        masked, allowed, rel_hot, query_hot = block_scores(block_start, queries)
        probs_f32 = jnp.exp(masked - lse_rows)
        grad_probs = jnp.einsum("ihe,jhe->hij", grad_context, values, preferred_element_type=f32)
        row_dot = jnp.sum(grad_probs * probs_f32, axis=-1, keepdims=True)
        grad_scores = jnp.where(allowed[None], probs_f32 * (grad_probs - row_dot), 0.0).astype(bf16)
        grad_query_rows = jnp.einsum(
            "hij,jhe->ihe", grad_scores, key_rows, preferred_element_type=f32
        )
        grad_key_rows = grad_key_rows + jnp.einsum(
            "hij,ihe->jhe", grad_scores, queries, preferred_element_type=f32
        )
        grad_value_rows = grad_value_rows + jnp.einsum(
            "hij,ihe->jhe", probs_f32.astype(bf16), grad_context, preferred_element_type=f32
        )
        grad_rel = grad_rel + lax.dot_general(
            grad_scores.reshape(HEADS, -1),
            rel_hot,
            (((1,), (1,)), ((), ())),
            preferred_element_type=f32,
        )
        query_sums = jnp.einsum("kia,hij->khaj", query_hot, grad_scores, preferred_element_type=f32)
        grad_layout = grad_layout + jnp.einsum(
            "khaj,kjb->khab", query_sums, pos_hot_f32, precision=highest
        )
        return ((grad_key_rows, grad_value_rows, grad_rel, grad_layout), grad_query_rows)

    start_state = (
        jnp.zeros((tok_count, HEADS, HEAD_DIM), f32),
        jnp.zeros((tok_count, HEADS, HEAD_DIM), f32),
        jnp.zeros((HEADS, BUCKETS), f32),
        jnp.zeros((2, HEADS, LAYOUT_POS, LAYOUT_POS), f32),
    )
    (grad_key_rows, grad_value_rows, grad_rel, grad_layout), grad_query_blocks = lax.scan(
        backward_block, start_state, (block_starts, lse_blocks)
    )
    grad_projected = jnp.stack(
        [
            grad_query_blocks.reshape(tok_count, model_width),
            grad_key_rows.reshape(tok_count, model_width),
            grad_value_rows.reshape(tok_count, model_width),
        ]
    ).astype(bf16)
    grad_qkv = jnp.einsum("td,kte->kde", normed_one, grad_projected, preferred_element_type=f32)
    grad_normed_one = jnp.einsum(
        "kte,kde->td", grad_projected, w_attn[:3], preferred_element_type=f32
    )
    unused_first, norm_pull_one = jax.vjp(scaled_norm, stream, gain_one)
    grad_stream, grad_gain_one = norm_pull_one(grad_normed_one)
    grad_tokens = grad_residual + grad_stream
    grad_layout_tables = jnp.dot(
        grad_layout.reshape(2 * HEADS, LAYOUT_POS * LAYOUT_POS), layout_hot.T, precision=highest
    ).reshape(2, HEADS, BUCKETS)
    grad_tables = jnp.concatenate([grad_rel[None], grad_layout_tables], 0)
    grad_small = jnp.concatenate(
        [grad_gain_one, grad_gain_two, jnp.transpose(grad_tables, (0, 2, 1)).reshape(-1)]
    )
    grad_attn = jnp.concatenate([grad_qkv, grad_out_proj[None]], 0)
    owned_attn, owned_in, owned_down, owned_small = (
        lax.psum_scatter(grad_attn, ("dp", "fsdp"), scatter_dimension=1, tiled=True),
        lax.psum_scatter(grad_in, ("dp", "fsdp"), scatter_dimension=1, tiled=True),
        lax.psum_scatter(grad_down, ("dp", "fsdp"), scatter_dimension=0, tiled=True),
        lax.psum_scatter(grad_small, ("dp", "fsdp"), scatter_dimension=0, tiled=True),
    )
    local_squares = (
        jnp.sum(owned_attn * owned_attn)
        + jnp.sum(owned_in * owned_in)
        + jnp.sum(owned_down * owned_down)
        + jnp.sum(owned_small * owned_small)
    )
    grad_norm = jnp.sqrt(lax.psum(local_squares, ("dp", "fsdp")))
    clip_scale = clip_max / jnp.maximum(grad_norm, clip_max)
    attn_new = adamw_update(
        attn_master, attn_first, attn_second, owned_attn * clip_scale, matrix_rate, decay_rate
    )
    ffin_new = adamw_update(
        ffin_master, ffin_first, ffin_second, owned_in * clip_scale, matrix_rate, decay_rate
    )
    down_new = adamw_update(
        down_master, down_first, down_second, owned_down * clip_scale, matrix_rate, decay_rate
    )
    small_new = adamw_update(
        small_master, small_first, small_second, owned_small * clip_scale, small_rate, 0.0
    )
    return (
        block_out,
        grad_tokens,
        grad_norm,
        attn_new[0],
        attn_new[1],
        attn_new[2][1:],
        attn_new[2][0],
        ffin_new[0],
        ffin_new[1],
        ffin_new[2],
        down_new[0],
        down_new[1],
        down_new[2],
        small_new[0],
        small_new[1],
        small_new[2],
    )


def solution(mesh):
    return jax.shard_map(
        on_device,
        mesh=mesh,
        in_specs=(
            P(("dp", "fsdp"), None),
            P(("dp", "fsdp"), None),
            P(None, ("dp", "fsdp")),
            P(None, ("dp", "fsdp")),
            P(None, ("dp", "fsdp"), None),
            P(None, ("dp", "fsdp"), None),
            P(None, ("dp", "fsdp"), None),
            P(None, ("dp", "fsdp"), None),
            P(None, ("dp", "fsdp"), None),
            P(None, ("dp", "fsdp"), None),
            P(("dp", "fsdp"), None),
            P(("dp", "fsdp"), None),
            P(("dp", "fsdp"), None),
            P(("dp", "fsdp")),
            P(("dp", "fsdp")),
            P(("dp", "fsdp")),
        ),
        out_specs=(
            P(("dp", "fsdp"), None),
            P(("dp", "fsdp"), None),
            P(),
            P(None, ("dp", "fsdp"), None),
            P(None, ("dp", "fsdp"), None),
            P(None, ("dp", "fsdp"), None),
            P(("dp", "fsdp"), None),
            P(None, ("dp", "fsdp"), None),
            P(None, ("dp", "fsdp"), None),
            P(None, ("dp", "fsdp"), None),
            P(("dp", "fsdp"), None),
            P(("dp", "fsdp"), None),
            P(("dp", "fsdp"), None),
            P(("dp", "fsdp")),
            P(("dp", "fsdp")),
            P(("dp", "fsdp")),
        ),
        check_vma=False,
    )
```

profile of v0, /device:TPU:0, one launch (start us, length us, event | category | flops | bytes accessed | tf_op | source)
XLA Modules:
  0.0 1311.5 jit_solution(7197656487361562181)
XLA Ops:
  13.7 42.5 %all-reduce = bf16[3584]{0:T(1024)(128)(2,1)S(1)} all-reduce(bf16[3584]{0:T(1024)(128)(2,1)S(1)} %dynamic-update-slice), channel_id=1, replica_groups=mesh['dp'=4,'fsdp'=8] {'dp','fsdp'}, use_global_device_ids=true, to_apply=%add | all-reduce | flops 3584 | bytes 14336
  58.8 6.2 fusion.2
  65.0 19.1 %copy.173 = f32[2,8,512,512]{3,2,1,0:T(8,128)} copy(f32[2,8,512,512]{3,1,2,0:T(8,128)S(1)} %bitcast.163) | data formatting | bytes 33554432
  84.1 17.8 %copy.141 = f32[16,512,512]{1,2,0:T(8,128)} copy(f32[16,512,512]{2,1,0:T(8,128)} %bitcast.164) | data formatting | bytes 33554432 | tf_op jit(solution)/shard_map/while/body/eval_jaxpr/reshape | solution.py:137
  105.1 7.4 fusion.47
  112.5 6.7 convert_bitcast_fusion
  125.2 19.0 %fusion.105 = (f32[16,512]{1,0:T(8,128)S(1)}, f32[16,512,512]{1,2,0:T(8,128)}) fusion(f32[16,512,512]{1,2,0:T(8,128)} %copy.141, f32[16,512,512,1]{1,2,3,0:T(8,128)} %fusion.47, bf16[512,16,64]{0,2,1:T(8,128)(2,1)S(1)} %bitcast.167, bf16[512,16,64]{0,2,1:T(8,128)(2,1)S(1)} %bitcast.165, pred[512,512]{0,1:T(8,128)(4,1)S(1)} %compare_and_fusion), kind=kOutput, calls=%fused_computation.157 | convolution fusion | flops 553639936 | bytes 52723712 | tf_op jit(solution)/shard_map/while/body/eval_jaxpr/ihe,jhe->hij/dot_general | solution.py:147
  144.2 9.9 fusion.10
  154.2 7.6 fusion.57
  166.4 18.9 %all-gather.6.cloned.1.call-done = bf16[2,1024,2816]{2,1,0:T(8,128)(2,1)} async-done(((bf16[2,32,2816]{2,1,0:T(8,128)(2,1)}), bf16[2,1024,2816]{2,1,0:T(8,128)(2,1)}) %all-gather.6.cloned.1.call-update) | async-done | bytes 11534352 | tf_op jit(solution)/shard_map/all_gather | solution.py:98
  185.4 12.6 convolution_bitcast_fusion.1
  198.0 56.6 %all-gather.8.cloned.1.call-done = bf16[1024,2816]{1,0:T(8,128)(2,1)} async-done(((bf16[32,2816]{1,0:T(8,128)(2,1)}), bf16[1024,2816]{1,0:T(8,128)(2,1)}) %all-gather.8.cloned.1.call-update) | async-done | bytes 5767184 | tf_op jit(solution)/shard_map/all_gather | solution.py:99
  254.5 13.1 %fusion.35 = (bf16[1,512,2816]{2,1,0:T(8,128)(2,1)}, bf16[1,512,2816]{2,1,0:T(8,128)(2,1)}, bf16[512,2816]{1,0:T(8,128)(2,1)}) fusion(f32[2,512,2816]{2,1,0:T(8,128)} %convolution_bitcast_fusion.1, bf16[1024,2816]{1,0:T(8,128)(2,1)} %all-gather.8.cloned.1.call-done, bf16[512,1024]{1,0:T(8,128)(2,1)S(1)} %copy-done.13, f32[512]{0:T(512)S(1)} %fusion.98), kind=kOutput, calls=%fused_computation.61 | convolution fusion | flops 2991849472 | bytes 27002880 | tf_op jit(solution)/shard_map/td,df->tf/dot_general | solution.py:181
  267.6 12.7 fusion.46
  289.7 9.4 fusion.59
  299.2 21.6 %select_convert_fusion = bf16[16,512,512]{1,2,0:T(8,128)(2,1)} fusion(f32[16,512,512]{1,2,0:T(8,128)} %get-tuple-element.193, f32[16,512]{1,0:T(8,128)S(1)} %log_add_fusion, pred[512,512]{0,1:T(8,128)(4,1)S(1)} %compare_and_fusion, bf16[512,16,64]{0,2,1:T(8,128)(2,1)S(1)} %bitcast.174, bf16[512,16,64]{0,2,1:T(8,128)(2,1)} %bitcast.175), kind=kOutput, calls=%fused_computation.8 | convolution fusion | flops 1103110656 | bytes 27557888 | tf_op jit(solution)/shard_map/while/body/eval_jaxpr/sub | solution.py:204
  320.8 7.1 convolution_convert_fusion.1
  334.6 11.1 convolution_bitcast_fusion
  350.8 5.9 convolution_bitcast_fusion.2
  356.8 6.2 pad_maximum_fusion
  363.0 20.2 %copy.152 = f32[4,1024,1024]{2,0,1:T(4,128)} copy(f32[4,1024,1024]{1,2,0:T(8,128)} %pad_maximum_fusion) | data formatting | bytes 33554432 | tf_op jit(solution)/shard_map/concatenate | solution.py:256
  383.2 34.1 %copy.154 = f32[2,1024,2816]{2,0,1:T(2,128)} copy(f32[2,1024,2816]{1,2,0:T(8,128)} %convolution_bitcast_fusion) | data formatting | bytes 46137344 | tf_op jit(solution)/shard_map/td,ktf->kdf/transpose | solution.py:185
  418.6 8.1 fusion.73
  427.3 6.5 fusion.14
  437.0 15.1 %copy.174 = bf16[2,8,512,512]{3,1,2,0:T(8,128)(2,1)} copy(bf16[2,8,512,512]{2,3,1,0:T(8,128)(2,1)} %bitcast.162) | data formatting | bytes 16777216
  452.7 8.0 fusion.62
  460.9 9.1 fusion.41
  470.0 41.6 %all-reduce.3 = f32[3584]{0:T(1024)S(1)} all-reduce(f32[3584]{0:T(1024)S(1)} %pad_maximum_fusion.7), channel_id=5, replica_groups=mesh['dp'=4,'fsdp'=8] {'dp','fsdp'}, use_global_device_ids=true, to_apply=%region_15.16.clone | all-reduce | flops 3584 | bytes 28672
  512.3 8.0 multiply_convert_fusion.2
  520.3 474.9 %all-reduce.7.cloned.1.call-done = (f32[4,1024,1024]{2,0,1:T(4,128)}, f32[2,1024,2816]{2,0,1:T(2,128)}) async-done(((f32[4,1024,1024]{2,0,1:T(4,128)}, f32[2,1024,2816]{2,0,1:T(2,128)}), (f32[4,1024,1024]{2,0,1:T(4,128)}, f32[2,1024,2816]{2,0,1:T(2,128)})) %all-reduce.7.cloned.1.call-update) | async-done | bytes 39845904
  1000.9 246.1 %reduce-scatter.2.cloned.1.call-done = f32[32,2816]{1,0:T(8,128)} async-done(((f32[1024,2816]{1,0:T(8,128)}), f32[32,2816]{1,0:T(8,128)}) %reduce-scatter.2.cloned.1.call-update) | async-done | bytes 360464 | tf_op jit(solution)/shard_map/reduce_scatter | solution.py:260
  1254.2 39.3 %psum.7 = f32[]{:T(128)} all-reduce(f32[]{:T(128)S(6)} %add.176), channel_id=1, replica_groups=mesh['dp'=4,'fsdp'=8] {'dp','fsdp'}, use_global_device_ids=true, to_apply=%region_17.18 | all-reduce | flops 1 | bytes 8 | tf_op jit(solution)/shard_map/psum | solution.py:269
  (129 shorter events, 68.5 us)
Async XLA Ops:
  7.2 105.4 %all-gather.4.cloned.1.call-start = ((), (), s32[]{:S(2)}) async-start(), calls=%async_computation.1 | async-start | bytes 8650752 | tf_op jit(solution)/shard_map/all_gather | solution.py:97
  9.0 176.3 %all-gather.6.cloned.1.call-start = ((), (), s32[]{:S(2)}) async-start(), calls=%async_computation.2 | async-start | bytes 11894784 | tf_op jit(solution)/shard_map/all_gather | solution.py:98
  11.0 243.5 %all-gather.8.cloned.1.call-start = ((), (), s32[]{:S(2)}) async-start(), calls=%async_computation.3 | async-start | bytes 5947392 | tf_op jit(solution)/shard_map/all_gather | solution.py:99
  12.7 982.5 %all-reduce.7.cloned.1.call-start = ((), (), s32[]{:S(2)}) async-start(), calls=%async_computation.5 | async-start | bytes 79691776
  84.1 17.8 %copy-start.24 = (s32[2,1]{0,1:T(1,128)S(1)}, s32[2,1]{0,1:T(1,128)}, u32[]{:S(2)}) copy-start(s32[2,1]{0,1:T(1,128)} %param.20) | copy-start | bytes 28
  84.1 20.4 %copy-start.5 = (bf16[512,1024]{1,0:T(8,128)(2,1)S(1)}, bf16[512,1024]{1,0:T(8,128)(2,1)}, u32[]{:S(2)}) copy-start(bf16[512,1024]{1,0:T(8,128)(2,1)} %param.18) | copy-start | bytes 3145732
  84.1 20.9 %copy-start.9 = (bf16[2,16,64,64]{3,2,1,0:T(8,128)(2,1)S(1)}, bf16[2,16,64,64]{3,2,1,0:T(8,128)(2,1)}, u32[]{:S(2)}) copy-start(bf16[2,16,64,64]{3,2,1,0:T(8,128)(2,1)} %convert_element_type.117) | copy-start | bytes 786436
  84.1 21.0 %copy-start.20 = (s32[2,512]{1,0:T(2,128)S(1)}, s32[2,512]{1,0:T(2,128)}, u32[]{:S(2)}) copy-start(s32[2,512]{1,0:T(2,128)} %param.21) | copy-start | bytes 12292
  104.8 7.8 copy-start.22
  144.2 9.9 copy-start.16
  161.8 4.6 copy-start.28
  185.3 69.2 %copy-start.13 = (bf16[512,1024]{1,0:T(8,128)(2,1)S(1)}, bf16[512,1024]{1,0:T(8,128)(2,1)}, u32[]{:S(2)}) copy-start(bf16[512,1024]{1,0:T(8,128)(2,1)} %param.19) | copy-start | bytes 3145732
  254.5 13.1 %copy-start.1 = (f32[512,1024]{1,0:T(8,128)S(1)}, f32[512,1024]{1,0:T(8,128)}, u32[]{:S(2)}) copy-start(f32[512,1024]{1,0:T(8,128)} %get-tuple-element.195) | copy-start | bytes 6291460
  320.8 7.1 copy-start
  329.8 3.4 copy-start.2
  329.8 3.4 copy-start.30
  329.8 4.8 copy-start.31
  350.8 6.0 copy-start.15
  350.8 6.0 copy-start.7
  417.4 829.6 %reduce-scatter.2.cloned.1.call-start = ((), (), s32[]{:S(2)}) async-start(), calls=%async_computation.4 | async-start | bytes 11894784 | tf_op jit(solution)/shard_map/reduce_scatter | solution.py:260
  437.0 15.1 %copy-start.10 = (f32[2,16,4096]{2,1,0:T(8,128)S(1)}, f32[2,16,4096]{2,1,0:T(8,128)}, u32[]{:S(2)}) copy-start(f32[2,16,4096]{2,1,0:T(8,128)} %dot_general.128) | copy-start | bytes 1572868
  437.0 15.1 %copy-start.17 = (f32[32,4096,1]{1,0,2:T(8,128)S(1)}, f32[32,4096,1]{1,0,2:T(8,128)}, u32[]{:S(2)}) copy-start(f32[32,4096,1]{1,0,2:T(8,128)} %constant.132) | copy-start | bytes 1572868
  452.7 8.2 copy-start.6
  460.9 51.4 %copy-start.23 = (f32[512]{0:T(512)S(1)}, f32[512]{0:T(512)}, u32[]{:S(2)}) copy-start(f32[512]{0:T(512)} %copy-done.22) | copy-start | bytes 6148
  1250.0 48.6 %copy-start.25 = (f32[112]{0:T(128)S(1)}, f32[112]{0:T(128)}, u32[]{:S(2)}) copy-start(f32[112]{0:T(128)} %param.31) | copy-start | bytes 1348
  1250.0 48.6 %copy-start.26 = (f32[112]{0:T(128)S(1)}, f32[112]{0:T(128)}, u32[]{:S(2)}) copy-start(f32[112]{0:T(128)} %param.32) | copy-start | bytes 1348
  1250.0 48.6 %copy-start.27 = (f32[112]{0:T(128)S(1)}, f32[112]{0:T(128)}, u32[]{:S(2)}) copy-start(f32[112]{0:T(128)} %param.33) | copy-start | bytes 1348
  1250.0 49.2 %copy-start.8 = (f32[2,32,2816]{2,1,0:T(8,128)S(1)}, f32[2,32,2816]{2,1,0:T(8,128)}, u32[]{:S(2)}) copy-start(f32[2,32,2816]{2,1,0:T(8,128)} %param.25) | copy-start | bytes 2162692
  1254.2 48.1 %copy-start.11 = (f32[32,2816]{1,0:T(8,128)S(1)}, f32[32,2816]{1,0:T(8,128)}, u32[]{:S(2)}) copy-start(f32[32,2816]{1,0:T(8,128)} %param.28) | copy-start | bytes 1081348
  1254.2 48.1 %copy-start.12 = (f32[32,2816]{1,0:T(8,128)S(1)}, f32[32,2816]{1,0:T(8,128)}, u32[]{:S(2)}) copy-start(f32[32,2816]{1,0:T(8,128)} %reduce-scatter.2.cloned.1.call-done) | copy-start | bytes 1081348
  1254.2 48.1 %copy-start.18 = (f32[32,2816]{1,0:T(8,128)S(1)}, f32[32,2816]{1,0:T(8,128)}, u32[]{:S(2)}) copy-start(f32[32,2816]{1,0:T(8,128)} %param.29) | copy-start | bytes 1081348
  1254.2 48.1 %copy-start.19 = (f32[32,2816]{1,0:T(8,128)S(1)}, f32[32,2816]{1,0:T(8,128)}, u32[]{:S(2)}) copy-start(f32[32,2816]{1,0:T(8,128)} %param.30) | copy-start | bytes 1081348
  (5 other events, 6.7 us)
Sparse Core Ops, SparseCore 0:
  11.7 80.2 all-gather.3
  95.4 89.8 all-gather.5
  188.8 65.6 all-gather.7
  417.5 577.6 all-reduce.6
  997.4 249.5 reduce-scatter.1
where the time goes:
time: 1320 us; the launch traced here: 1310 us
  waiting for transfers between devices  797 us (60%)
  matrix products  197 us (15%)
  local copies, waits for them, and re-layouts  129 us (10%)
  blocking collectives  123 us (9%)
  other arithmetic  44.3 us (3%)
  between operations  20.4 us (2%)
    unnamed x6, waiting for transfers between devices  475 us
    reduce_scatter x1, waiting for transfers between devices, on_device(): lax.psum_scatter(grad_down, ('dp', 'fsdp'), scatter_dimension=0, tiled=True)  246 us
    unnamed x2, blocking collectives  84.1 us
    all_gather x1, waiting for transfers between devices, on_device(): lax.all_gather(down_low, ('dp', 'fsdp'), axis=0, tiled=True)  56.6 us
    unnamed x68, local copies, waits for them, and re-layouts  39.4 us
    psum x1, blocking collectives, on_device(): grad_norm = jnp.sqrt(lax.psum(local_squares, ('dp', 'fsdp')))  39.3 us
    transpose x1, local copies, waits for them, and re-layouts, on_device(): jnp.einsum('td,ktf->kdf', normed_two, grad_gate_up, preferred_element_typ...  34.1 us
  transfers between devices with their start and end apart: 5, of which 4 were waited for; matrix products, arithmetic and copies ran while one was open for 14% of the time, Pallas kernels for 0%

commit v1 on v0

--- a/solution.py
+++ b/solution.py
@@ -1,7 +1,11 @@
+import functools
+
 import jax
 import jax.numpy as jnp
 import numpy as np
 from jax import lax
+from jax.experimental import pallas as pl
+from jax.experimental.pallas import tpu as pltpu
 from jax.sharding import PartitionSpec as P
 
 HEADS = 16
@@ -300,9 +304,1079 @@
     )
 
 
-def solution(mesh):
+MESH = pl.DeviceIdType.MESH
+TILE = 256
+HALF = 16
+SLOTS = 4
+VMEM_BYTES = 63 * 2**20
+QKV_GROUPS = 4
+OUT_GROUPS = 2
+OUT_START = 12
+FF_START = 16
+
+
+def bucket_limits(tok_count):
+    buckets = relative_buckets(tok_count, BUCKETS)[:, 0]
+    return [int(np.argmax(buckets >= k)) for k in range(1, BUCKETS // 2)]
+
+
+def dot(a, b):
+    return lax.dot_general(a, b, (((1,), (0,)), ((), ())), preferred_element_type=jnp.float32)
+
+
+def dot_nt(a, b):
+    return lax.dot_general(a, b, (((1,), (1,)), ((), ())), preferred_element_type=jnp.float32)
+
+
+def split_dot(a, b):
+    high = a.astype(jnp.bfloat16)
+    rest = (a - high.astype(jnp.float32)).astype(jnp.bfloat16)
+    return dot(high, b) + dot(rest, b)
+
+
+def iota(shape, dim):
+    return lax.broadcasted_iota(jnp.int32, shape, dim)
+
+
+def layer_kernel(
+    sizes,
+    page_ref,
+    pos_ref,
+    small_ref,
+    tok_hbm,
+    cot_hbm,
+    attn_hbm,
+    ffin_hbm,
+    down_hbm,
+    out_ref,
+    gtok_ref,
+    oattn_ref,
+    oin_ref,
+    odown_ref,
+    osmall_ref,
+    norm_ref,
+    w,
+    rh,
+    rd,
+    re,
+    rf,
+    own,
+    smb,
+    sga,
+    sgr,
+    sgz,
+    nbr,
+    nbz,
+    tok,
+    n1,
+    n1t,
+    qp,
+    kp,
+    vp,
+    ctx,
+    ctxt,
+    res,
+    n2,
+    n2t,
+    gout,
+    goutt,
+    gn,
+    gctx,
+    kxs,
+    km,
+    gv,
+    lse,
+    ggv,
+    ggx,
+    ggy,
+    acc,
+    hx,
+    hxx,
+    hq2,
+    k2,
+    hxt,
+    hyt,
+    dq,
+    dk,
+    dv,
+    gains,
+    gsum,
+    load_sem,
+    in_sem,
+    ag_send,
+    ag_recv,
+    rs_send,
+    rs_recv,
+    sm_send,
+    sm_recv,
+):
+    ny, nz, nx, per, ff_groups = sizes
+    f32, bf16 = jnp.float32, jnp.bfloat16
+    groups = QKV_GROUPS + OUT_GROUPS + ff_groups
+    tok_count, width = tok.shape
+    rows = w.shape[5]
+    dp, fs = lax.axis_index("dp"), lax.axis_index("fsdp")
+    y, c, z, x = dp // 2, dp % 2, fs // nx, fs % nx
+
+    def device(yy, cc, zz, xx):
+        return (yy * 2 + cc, zz * nx + xx)
+
+    sib, xnb, ynb = device(y, 1 - c, z, x), device(y, c, z, 1 - x), device(1 - y, c, z, x)
+
+    def zdev(k):
+        return device(y, c, lax.rem(z + k, nz), x)
+
+    def remote(src, dst, send, recv, dev):
+        return pltpu.make_async_remote_copy(
+            src_ref=src, dst_ref=dst, send_sem=send, recv_sem=recv, device_id=dev, device_id_type=MESH
+        )
+
+    barrier = pltpu.get_barrier_semaphore()
+    for dev in [sib, xnb, ynb] + [zdev(k) for k in range(1, nz)]:
+        pl.semaphore_signal(barrier, inc=1, device_id=dev, device_id_type=MESH)
+
+    def on_group(g, fn):
+        if isinstance(g, int):
+            if 0 <= g < groups:
+                if g < QKV_GROUPS:
+                    fn(3 * g, 3, g)
+                elif g < QKV_GROUPS + OUT_GROUPS:
+                    fn(OUT_START + 2 * (g - QKV_GROUPS), 2, g)
+                else:
+                    fn(FF_START + 3 * (g - QKV_GROUPS - OUT_GROUPS), 3, g)
+            return
+        is_out = jnp.logical_and(g >= QKV_GROUPS, g < QKV_GROUPS + OUT_GROUPS)
+        inside = jnp.logical_and(g >= 0, g < groups)
+
+        @pl.when(is_out)
+        def _():
+            fn(OUT_START + 2 * (g - QKV_GROUPS), 2, g)
+
+        @pl.when(jnp.logical_and(inside, jnp.logical_not(is_out)))
+        def _():
+            fn(jnp.where(g < QKV_GROUPS, 3 * g, FF_START + 3 * (g - QKV_GROUPS - OUT_GROUPS)), 3, g)
+
+    def load(g):
+        def go(t0, count, g):
+            if count == 2:
+                for i in range(2):
+                    cols = pl.ds(pl.multiple_of((t0 - OUT_START + i) * TILE, TILE), TILE)
+                    pltpu.make_async_copy(attn_hbm.at[3, :, cols], own.at[t0 + i], load_sem.at[g]).start()
+            elif isinstance(g, int) and g < QKV_GROUPS:
+                cols = pl.ds(g * TILE, TILE)
+                pltpu.make_async_copy(
+                    attn_hbm.at[pl.ds(0, 3), :, cols], own.at[pl.ds(t0, 3)], load_sem.at[g]
+                ).start()
+            else:
+                cols = pl.ds((g - QKV_GROUPS - OUT_GROUPS) * TILE, TILE)
+                pltpu.make_async_copy(
+                    ffin_hbm.at[:, :, cols], own.at[pl.ds(t0, 2)], load_sem.at[g]
+                ).start()
+                pltpu.make_async_copy(down_hbm.at[:, cols], own.at[t0 + 2], load_sem.at[g]).start()
+
+        on_group(g, go)
+
+    def load_wait(g):
+        def go(t0, count, g):
+            tiles = own.at[pl.ds(t0, count)]
+            pltpu.make_async_copy(tiles, tiles, load_sem.at[g]).wait()
+            for i in range(count):
+                w[t0 + i, y, c, z, x] = own[t0 + i].astype(bf16)
+
+        on_group(g, go)
+
+    for g in range(groups):
+        load(g)
+    tok_copy = pltpu.make_async_copy(tok_hbm, tok, in_sem.at[0])
+    cot_copy = pltpu.make_async_copy(cot_hbm, gout, in_sem.at[1])
+    tok_copy.start()
+    cot_copy.start()
+
+    def ag_parts(t0, count, g):
+        t = pl.ds(t0, count)
+        return t, (lambda i: ag_send.at[i, g]), (lambda i: ag_recv.at[i, g])
+
+    def ag1(g):
+        def go(t0, count, g):
+            t, s, r = ag_parts(t0, count, g)
+            mine = w.at[t, y, c, z, x]
+            for k in range(1, nz):
+                remote(mine, mine, s(0), r(0), zdev(k)).start()
+
+        on_group(g, go)
+
+    def ag2(g):
+        def go(t0, count, g):
+            t, s, r = ag_parts(t0, count, g)
+            three = w.at[t, y, c, pl.ds(0, nz - 1), x]
+            remote(three, three, s(0), r(0), zdev(1)).wait_recv()
+            column = w.at[t, y, c, :, x]
+            remote(column, column, s(1), r(1), xnb).start()
+            remote(column, column, s(2), r(2), ynb).start()
+            remote(column, column, s(5), r(5), sib).start()
+
+        on_group(g, go)
+
+    def ag3(g):
+        def go(t0, count, g):
+            t, s, r = ag_parts(t0, count, g)
+            xcol = w.at[t, y, c, :, 1 - x]
+            ycol = w.at[t, 1 - y, c, :, x]
+            remote(xcol, xcol, s(1), r(1), xnb).wait_recv()
+            xhalf = w.at[t, y, c, :, 1 - x, pl.ds(0, HALF)]
+            remote(xhalf, xhalf, s(4), r(4), ynb).start()
+            remote(xcol, xcol, s(5), r(5), sib).start()
+            remote(ycol, ycol, s(2), r(2), ynb).wait_recv()
+            yhalf = w.at[t, 1 - y, c, :, x, pl.ds(HALF, HALF)]
+            remote(yhalf, yhalf, s(3), r(3), xnb).start()
+            remote(ycol, ycol, s(5), r(5), sib).start()
+
+        on_group(g, go)
+
+    def ag4(g):
+        def go(t0, count, g):
+            t, s, r = ag_parts(t0, count, g)
+            low = w.at[t, 1 - y, c, :, 1 - x, pl.ds(0, HALF)]
+            high = w.at[t, 1 - y, c, :, 1 - x, pl.ds(HALF, HALF)]
+            remote(low, low, s(4), r(4), ynb).wait_recv()
+            remote(high, high, s(3), r(3), xnb).wait_recv()
+            diag = w.at[t, 1 - y, c, :, 1 - x]
+            remote(diag, diag, s(5), r(5), sib).start()
+
+        on_group(g, go)
+
+    def ag5(g):
+        def go(t0, count, g):
+            t, s, r = ag_parts(t0, count, g)
+            plane = w.at[t, :, 1 - c]
+            remote(plane, plane, s(5), r(5), sib).wait_recv()
+
+        on_group(g, go)
+
+    def ag_sent(g):
+        def go(t0, count, g):
+            t, s, r = ag_parts(t0, count, g)
+            three = w.at[t, y, c, pl.ds(0, nz - 1), x]
+            column = w.at[t, y, c, :, x]
+            half = w.at[t, y, c, :, x, pl.ds(0, HALF)]
+            plane = w.at[t, :, c]
+            remote(three, three, s(0), r(0), zdev(1)).wait_send()
+            remote(column, column, s(1), r(1), xnb).wait_send()
+            remote(column, column, s(2), r(2), ynb).wait_send()
+            remote(half, half, s(3), r(3), xnb).wait_send()
+            remote(half, half, s(4), r(4), ynb).wait_send()
+            remote(plane, plane, s(5), r(5), sib).wait_send()
+
+        on_group(g, go)
+
+    def ag_tick(t):
+        ag2(t)
+        ag3(t - 1)
+        ag4(t - 2)
+        ag5(t - 3)
+
+    def rs_group(n):
+        if isinstance(n, int):
+            if n < 0 or n >= groups:
+                return -1
+            tail = n - ff_groups
+            if tail < 0:
+                return QKV_GROUPS + OUT_GROUPS + n
+            return QKV_GROUPS + tail if tail < OUT_GROUPS else tail - OUT_GROUPS
+        tail = n - ff_groups
+        g = jnp.where(
+            tail < 0,
+            QKV_GROUPS + OUT_GROUPS + n,
+            jnp.where(tail < OUT_GROUPS, QKV_GROUPS + tail, tail - OUT_GROUPS),
+        )
+        return jnp.where(jnp.logical_or(n < 0, n >= groups), -1, g)
+
+    def on_sum(n, fn):
+        slot = n % SLOTS if isinstance(n, int) else lax.rem(n + SLOTS, SLOTS)
+
+        def go(t0, count, g):
+            fn(t0, count, slot, (lambda i: rs_send.at[i, g]), (lambda i: rs_recv.at[i, g]))
+
+        on_group(rs_group(n), go)
+
+    def rs0(n):
+        def go(t0, count, slot, s, r):
+            remote(
+                w.at[pl.ds(t0, count), :, 1 - c], rh.at[slot, pl.ds(0, count)], s(0), r(0), sib
+            ).start()
+
+        on_sum(n, go)
+
+    def rs1(n):
+        def go(t0, count, slot, s, r):
+            t = pl.ds(t0, count)
+            landed = rh.at[slot, pl.ds(0, count)]
+            remote(w.at[t, :, 1 - c], landed, s(0), r(0), sib).wait_recv()
+
+            def add(i, carry):
+                for yy in range(ny):
+                    w[t0 + i, yy, c] = w[t0 + i, yy, c] + rh[slot, i, yy]
+                return carry
+
+            lax.fori_loop(0, count, add, 0)
+            for k, dev in ((0, xnb), (1, ynb)):
+                remote(
+                    w.at[t, 1 - y, c, :, 1 - x, pl.ds(k * HALF, HALF)],
+                    rd.at[slot, k, pl.ds(0, count)],
+                    s(1 + k),
+                    r(1 + k),
+                    dev,
+                ).start()
+
+        on_sum(n, go)
+
+    def rs2(n):
+        def go(t0, count, slot, s, r):
+            t = pl.ds(t0, count)
+            for k, dev, yy, xx in ((0, xnb, 1 - y, x), (1, ynb, y, 1 - x)):
+                landed = rd.at[slot, k, pl.ds(0, count)]
+                rows_k = pl.ds(k * HALF, HALF)
+                remote(w.at[t, 1 - y, c, :, 1 - x, rows_k], landed, s(1 + k), r(1 + k), dev).wait_recv()
+                for i in range(count):
+                    w[t0 + i, yy, c, :, xx, rows_k] = w[t0 + i, yy, c, :, xx, rows_k] + rd[slot, k, i]
+            for k, dev, yy, xx in ((0, xnb, y, 1 - x), (1, ynb, 1 - y, x)):
+                remote(
+                    w.at[t, yy, c, :, xx], re.at[slot, k, pl.ds(0, count)], s(3 + k), r(3 + k), dev
+                ).start()
+
+        on_sum(n, go)
+
+    def rs3(n):
+        def go(t0, count, slot, s, r):
+            t = pl.ds(t0, count)
+            for k, dev in ((0, xnb), (1, ynb)):
+                landed = re.at[slot, k, pl.ds(0, count)]
+                remote(w.at[t, y, c, :, x], landed, s(3 + k), r(3 + k), dev).wait_recv()
+            for i in range(count):
+                total = (
+                    w[t0 + i, y, c, z, x].astype(f32)
+                    + re[slot, 0, i, z].astype(f32)
+                    + re[slot, 1, i, z].astype(f32)
+                )
+                own[t0 + i] = total
+                for zz in range(nz):
+                    w[t0 + i, y, c, zz, x] = (
+                        w[t0 + i, y, c, zz, x].astype(f32)
+                        + re[slot, 0, i, zz].astype(f32)
+                        + re[slot, 1, i, zz].astype(f32)
+                    ).astype(bf16)
+            for k in range(1, nz):
+                remote(
+                    w.at[t, y, c, lax.rem(z + k, nz), x],
+                    rf.at[slot, k - 1, pl.ds(0, count)],
+                    s(5),
+                    r(5),
+                    zdev(k),
+                ).start()
+
+        on_sum(n, go)
+
+    def rs4(n):
+        def go(t0, count, slot, s, r):
+            landed = rf.at[slot, :, pl.ds(0, count)]
+            remote(landed, landed, s(5), r(5), zdev(1)).wait_recv()
+            for i in range(count):
+                total = own[t0 + i]
+                for k in range(nz - 1):
+                    total = total + rf[slot, k, i].astype(f32)
+                own[t0 + i] = total
+
+        on_sum(n, go)
+
+    def rs_sent(g):
+        def go(t0, count, g):
+            t = pl.ds(t0, count)
+            s, r = (lambda i: rs_send.at[i, g]), (lambda i: rs_recv.at[i, g])
+            plane = w.at[t, :, c]
+            half = w.at[t, y, c, :, x, pl.ds(0, HALF)]
+            column = w.at[t, y, c, :, x]
+            three = w.at[t, y, c, pl.ds(0, nz - 1), x]
+            for i, part in enumerate((plane, half, half, column, column, three)):
+                remote(part, part, s(i), r(i), sib).wait_send()
+
+        on_group(g, go)
+
+    def rs_tick(n):
+        rs0(n)
+        rs1(n - 1)
+        rs2(n - 2)
+        rs3(n - 3)
+        rs4(n - 4)
+
+    sm_steps = (
+        (smb.at[y, c, z, x], None),
+        (smb.at[y, c, :, x], xnb),
+        (smb.at[y, c], ynb),
+        (smb.at[:, c], sib),
+    )
+
+    def sm_start(i):
+        part, dev = sm_steps[i]
+        if i == 0:
+            for k in range(1, nz):
+                remote(part, part, sm_send.at[0], sm_recv.at[0], zdev(k)).start()
+        else:
+            remote(part, part, sm_send.at[i], sm_recv.at[i], dev).start()
+
+    def sm_wait(i):
+        part = (
+            smb.at[y, c, pl.ds(0, nz - 1), x],
+            smb.at[y, c, :, 1 - x],
+            smb.at[1 - y, c],
+            smb.at[:, 1 - c],
+        )[i]
+        dev = zdev(1) if i == 0 else sm_steps[i][1]
+        copy = remote(part, part, sm_send.at[i], sm_recv.at[i], dev)
+        copy.wait_recv()
+        copy.wait_send()
+
+    smb[y, c, z, x] = jnp.zeros(smb.shape[4:], f32)
+    smb[y, c, z, x, 0:1, 0:per] = small_ref[...].astype(bf16).astype(f32)
+    load_wait(0)
+    pl.semaphore_wait(barrier, 3 + nz - 1)
+    sm_start(0)
+    ag1(0)
+    for g in range(1, groups):
+        load_wait(g)
+        ag1(g)
+
+    lane = iota((tok_count, 128), 1)
+    row = iota((tok_count, 128), 0)
+    first_len = page_ref[0, 0]
+    both_len = page_ref[0, 0] + page_ref[1, 0]
+
+    def pos_rows(k):
+        line = pos_ref[k : k + 1, :].astype(f32)
+        return jnp.broadcast_to(line, (128, tok_count)).T.astype(jnp.int32)
+
+    pos_x, pos_y = pos_rows(0), pos_rows(1)
+    hot_x = (pos_x == lane).astype(f32)
+    hot_y = (pos_y == lane).astype(f32)
+    page = jnp.where(row < first_len, 0, jnp.where(row < both_len, 1, 2))
+    hx[...] = hot_x.astype(bf16)
+    hxx[...] = (pos_x == lax.rem(lane, 64)).astype(f32).astype(bf16)
+    hq2[...] = jnp.where(lane < 64, hot_y, (page == lane - 64).astype(f32)).astype(bf16)
+    barred = jnp.where(jnp.logical_and(page == lane - 64, page < 2), 0.0, far_negative)
+    k2[...] = jnp.where(lane < 64, hot_y, jnp.where(lane < 67, barred, 0.0)).astype(bf16)
+    hxt[...] = hot_x.T[0:64].astype(bf16)
+    hyt[...] = hot_y.T[0:64].astype(bf16)
+    sm_wait(0)
+    sm_start(1)
+    ag_tick(0)
+    cot_copy.wait()
+
+    def mask_out(i, carry):
+        at = pl.ds(pl.multiple_of(i * 128, 128), 128)
+        valid = (iota((128, width), 0) + i * 128 < both_len).astype(f32)
+        masked = valid * gout[at, :].astype(f32)
+        gout[at, :] = masked.astype(bf16)
+        goutt[:, at] = masked.T.astype(bf16)
+        return carry
+
+    lax.fori_loop(0, tok_count // 128, mask_out, 0)
+    sm_wait(1)
+    sm_start(2)
+    ag_tick(1)
+    sm_wait(2)
+    sm_start(3)
+    sm_wait(3)
+
+    devs = [(a, b, d, e) for a in range(ny) for b in range(2) for d in range(nz) for e in range(nx)]
+    lane1 = iota((1, 128), 1)
+
+    def flat_tile(n):
+        tile = jnp.zeros((1, 128), f32)
+        for d in range(128 * n // per, (128 * n + 127) // per + 1):
+            shift = d * per - 128 * n
+            line = smb[devs[d] + (slice(0, 1), slice(None))]
+            line = pltpu.roll(line, shift % 128, 1)
+            inside = jnp.logical_and(lane1 >= shift, lane1 < shift + per)
+            tile = jnp.where(inside, line, tile)
+        return tile
+
+    for n in range(2 * width // 128):
+        gains[n // (width // 128), :, pl.ds(128 * (n % (width // 128)), 128)] = flat_tile(n)
+    first_table = 2 * width // 128
+
+    def table(k):
+        flat = jnp.concatenate([flat_tile(first_table + 4 * k + i) for i in range(4)], axis=1)
+        keep = lax.rem(iota((HEADS, 512), 1), HEADS) == iota((HEADS, 512), 0)
+        return jnp.where(keep, jnp.broadcast_to(flat, (HEADS, 512)), 0.0).astype(bf16)
+
+    def hot(bucket_line, count):
+        return (iota((512, count), 0) // HEADS == bucket_line).astype(f32).astype(bf16)
+
+    limits = bucket_limits(tok_count)
+    span = 2 * tok_count
+
+    def rel_bucket(offset):
+        distance = jnp.abs(offset)
+        bucket = jnp.where(offset > 0, BUCKETS // 2, 0)
+        for limit in limits:
+            bucket = bucket + (distance >= limit).astype(jnp.int32)
+        return bucket
+
+    def layout_bucket(offset):
+        return jnp.clip(offset, -(BUCKETS // 2), BUCKETS // 2 - 1) + BUCKETS // 2
+
+    rel_values = dot(table(0), hot(rel_bucket(tok_count - iota((1, span), 1)), span))
+    for h in range(HEADS):
+        gv[h, 0:1, :] = rel_values[h : h + 1]
+    turned = jnp.where(lane1 < 64, lane1, lane1 - 128)
+    x_even = dot(table(1), hot(layout_bucket(lane1 - 64), 128))
+    x_odd = dot(table(1), hot(layout_bucket(turned), 128))
+    y_any = dot(table(2), hot(layout_bucket(turned), 128))
+    sq_lane, sq_row = iota((128, 128), 1), iota((128, 128), 0)
+
+    def slope(line):
+        return pltpu.roll(jnp.broadcast_to(line, (128, line.shape[1])), 0, 1, stride=1, stride_axis=0)
+
+    for p in range(HEADS // 2):
+        a, b = 2 * p, 2 * p + 1
+        both = jnp.where(sq_lane < 64, slope(x_odd[b : b + 1]), slope(x_even[a : a + 1]))
+        kxs[p] = jnp.where(sq_row < 64, both, 0.0).astype(bf16)
+        for h in (a, b):
+            part = jnp.where(sq_lane < 64, slope(y_any[h : h + 1]), 0.0)
+            km[h] = jnp.where(sq_row < 64, part, (sq_lane == sq_row).astype(f32)).astype(bf16)
+
+    tok_copy.wait()
+
+    def norm_one(i, carry):
+        at = pl.ds(pl.multiple_of(i * 128, 128), 128)
+        stream = tok[at, :].astype(f32)
+        scale = lax.rsqrt(jnp.mean(stream * stream, axis=-1, keepdims=True) + norm_eps)
+        low = (stream * scale * gains[0]).astype(bf16)
+        n1[at, :] = low
+        n1t[:, at] = low.astype(f32).T.astype(bf16)
+        return carry
+
+    lax.fori_loop(0, tok_count // 128, norm_one, 0)
+    ag_tick(2)
+
+    def tile_of(t):
+        return w[t].reshape(width, TILE)
+
+    half_lane = iota((tok_count, 128), 1) < 64
+
+    def pick(low, high):
+        return jnp.where(half_lane, low.astype(f32), high.astype(f32)).astype(bf16)
+
+    def augmented(p, e):
+        shift = dot(hx[...], kxs[p])
+        q_own, k_own = qp[p], kp[p]
+        q_first = pick(q_own, shift) if e == 0 else pick(shift, q_own)
+        k_first = pick(k_own, hxx[...]) if e == 0 else pick(hxx[...], k_own)
+        q_second = dot(hq2[...], km[2 * p + e]).astype(bf16)
+        return (
+            jnp.concatenate([q_first, q_second], axis=1),
+            jnp.concatenate([k_first, k2[...]], axis=1),
+        )
+
+    blocks = tok_count // 128
+    half_rows = tok_count // 2
+
+    def rel_bias(steep, part):
+        return jnp.concatenate(
+            [
+                steep[:, tok_count - 128 * jb + half_rows * part : tok_count - 128 * jb + half_rows * (part + 1)]
+                for jb in range(blocks)
+            ],
+            axis=0,
+        )
+
+    def forward_pair(p):
+        v_turned = vp[p].astype(f32).T.astype(bf16)
+        pieces = []
+        for e in range(2):
+            q_all, k_all = augmented(p, e)
+            steep = slope(gv[2 * p + e, 0:1, :])
+            parts = []
+            for part in range(2):
+                cols = slice(half_rows * part, half_rows * (part + 1))
+                scores = dot_nt(k_all, q_all[cols]) + rel_bias(steep, part)
+                top = jnp.max(scores, axis=0, keepdims=True)
+                exponent = jnp.exp(scores - top)
+                total = jnp.sum(exponent, axis=0, keepdims=True)
+                probs = (exponent * (1.0 / total)).astype(bf16)
+                lse[2 * p + e, 0:1, cols] = top + jnp.log(total)
+                parts.append(dot(v_turned[64 * e : 64 * (e + 1)], probs))
+            pieces.append(jnp.concatenate(parts, axis=1))
+        turned = jnp.concatenate(pieces, axis=0)
+        at = pl.ds(pl.multiple_of(p * 128, 128), 128)
+        ctxt[at, :] = turned.astype(bf16)
+        ctx[:, at] = turned.T.astype(bf16)
+
+    def project(j):
+        for i, dest in enumerate((qp, kp, vp)):
+            result = dot(n1[...], tile_of(3 * j + i)).astype(bf16)
+            dest[2 * j] = result[:, 0:128]
+            dest[2 * j + 1] = result[:, 128:256]
+
+    def forward_heads(j, carry):
+        ag_tick(j + 3)
+        project(j)
+
+        def one(i, inner):
+            forward_pair(2 * j + i)
+            return inner
+
+        lax.fori_loop(0, 2, one, 0)
+        return carry
+
+    lax.fori_loop(0, QKV_GROUPS, forward_heads, 0)
+    ag_tick(7)
+    ag_tick(8)
+
+    for e in range(4):
+        cols = pl.ds(e * TILE, TILE)
+        res[:, cols] = tok[:, cols].astype(f32) + dot(ctx[...], tile_of(OUT_START + e))
+
+    mix = gtok_ref
+
+    def norm_two(i, carry):
+        at = pl.ds(pl.multiple_of(i * 128, 128), 128)
+        stream = res[at, :]
+        scale = lax.rsqrt(jnp.mean(stream * stream, axis=-1, keepdims=True) + norm_eps)
+        low = (stream * scale * gains[1]).astype(bf16)
+        n2[at, :] = low
+        n2t[:, at] = low.astype(f32).T.astype(bf16)
+        mix[at, :] = stream
+        gn[at, :] = jnp.zeros((128, width), f32)
+        return carry
+
+    lax.fori_loop(0, tok_count // 128, norm_two, 0)
+
+    root = float(np.sqrt(2.0 / np.pi))
+
+    def feed(f, carry):
+        ag_tick(f + 9)
+        t0 = FF_START + 3 * f
+        gate_w, up_w, down_w = tile_of(t0), tile_of(t0 + 1), tile_of(t0 + 2)
+        gate = dot(n2[...], gate_w)
+        up = dot(n2[...], up_w)
+        grad_hidden = dot(gout[...], down_w)
+        square = gate * gate
+        turn = jnp.tanh(root * gate * (1.0 + 0.044715 * square))
+        half = 0.5 * (1.0 + turn)
+        active = gate * half
+        slope_of = half + 0.5 * gate * (1.0 - turn * turn) * (root * (1.0 + 3 * 0.044715 * square))
+        hidden = (active * up).astype(bf16)
+        grad_gate = (grad_hidden * up * slope_of).astype(bf16)
+        grad_up = (grad_hidden * active).astype(bf16)
+        mix[...] += dot_nt(hidden, down_w)
+        gn[...] += dot_nt(grad_gate, gate_w) + dot_nt(grad_up, up_w)
+        ag_sent(f + QKV_GROUPS + OUT_GROUPS)
+        shape = w.shape[1:]
+        w[t0] = dot(n2t[...], grad_gate).astype(bf16).reshape(shape)
+        w[t0 + 1] = dot(n2t[...], grad_up).astype(bf16).reshape(shape)
+        w[t0 + 2] = dot(goutt[...], hidden).astype(bf16).reshape(shape)
+        rs_tick(f)
+        return carry
+
+    lax.fori_loop(0, ff_groups, feed, 0)
+
+    gsum[...] = jnp.zeros_like(gsum)
+    grad_res = mix
+
+    def norm_two_back(i, carry):
+        at = pl.ds(pl.multiple_of(i * 128, 128), 128)
+        valid = (iota((128, width), 0) + i * 128 < both_len).astype(f32)
+        out_ref[at, :] = (valid * mix[at, :]).astype(bf16)
+        stream = res[at, :]
+        scale = lax.rsqrt(jnp.mean(stream * stream, axis=-1, keepdims=True) + norm_eps)
+        got = gn[at, :]
+        gsum[1] += jnp.sum((got * stream * scale).reshape(16, 8, width), axis=0)
+        scaled = gains[1] * got
+        inner = jnp.mean(scaled * stream, axis=-1, keepdims=True)
+        total = gout[at, :].astype(f32) + scale * scaled - stream * (scale * scale * scale * inner)
+        grad_res[at, :] = total
+        n2[at, :] = total.astype(bf16)
+        gn[at, :] = jnp.zeros((128, width), f32)
+        return carry
+
+    lax.fori_loop(0, tok_count // 128, norm_two_back, 0)
+    attended = n2
+    shape = w.shape[1:]
+    for yy in range(ny):
+        for cc in range(2):
+            part = jnp.zeros((tok_count, TILE), f32)
+            for e in range(4):
+                block = w[OUT_START + e, yy, cc].reshape(TILE, TILE)
+                part = part + dot_nt(attended[:, pl.ds(e * TILE, TILE)], block)
+            gctx[:, pl.ds((yy * 2 + cc) * TILE, TILE)] = part.astype(bf16)
+    for i in range(OUT_GROUPS):
+        ag_sent(QKV_GROUPS + i)
+        for e in (2 * i, 2 * i + 1):
+            w[OUT_START + e] = (
+                dot(ctxt[...], attended[:, pl.ds(e * TILE, TILE)]).astype(bf16).reshape(shape)
+            )
+        rs_tick(ff_groups + i)
+
+    flip = (sq_row + sq_lane == 127).astype(f32).astype(bf16)
+    flip_halves = jnp.where(
+        (sq_row < 64) == (sq_lane < 64), (lax.rem(sq_row, 64) + lax.rem(sq_lane, 64) == 63).astype(f32), 0.0
+    ).astype(bf16)
+
+    def split_left(matrix, value):
+        high = value.astype(bf16)
+        rest = (value - high.astype(f32)).astype(bf16)
+        return dot(matrix, high) + dot(matrix, rest)
+
+    def backward_pair(p, local):
+        at = pl.ds(pl.multiple_of(p * 128, 128), 128)
+        k_turned = kp[p].astype(f32).T.astype(bf16)
+        grad_rows = gctx[:, at]
+        dv_parts, dk_parts, dq_parts, x_parts, y_parts = [], [], [], [], []
+        for e in range(2):
+            h = 2 * p + e
+            q_all, k_all = augmented(p, e)
+            steep = slope(gv[h, 0:1, :])
+            zero = jnp.zeros((tok_count, 128), f32)
+            one_head = pick(grad_rows, zero) if e == 0 else pick(zero, grad_rows)
+            left = jnp.concatenate([k_turned[64 * e : 64 * (e + 1)], hxt[...], hyt[...]], axis=0)
+            acc[...] = jnp.zeros_like(acc)
+            dv_e = jnp.zeros((tok_count, 128), f32)
+            dk_e = jnp.zeros((tok_count, 128), f32)
+            turned = []
+            for part in range(2):
+                cols = slice(half_rows * part, half_rows * (part + 1))
+                scores = dot_nt(k_all, q_all[cols]) + rel_bias(steep, part)
+                probs = jnp.exp(scores - lse[h, 0:1, cols])
+                grad_probs = dot_nt(vp[p], one_head[cols])
+                inner = jnp.sum(grad_probs * probs, axis=0, keepdims=True)
+                grad_scores = (probs * (grad_probs - inner)).astype(bf16)
+                dv_e = dv_e + dot(probs.astype(bf16), grad_rows[cols])
+                dk_e = dk_e + dot(grad_scores, qp[p, cols])
+                turned.append(dot(left, grad_scores))
+                for jb in range(blocks):
+                    start = tok_count - 128 * jb + half_rows * part
+                    acc[:, start : start + half_rows] += grad_scores[128 * jb : 128 * (jb + 1)].astype(f32)
+            all_turned = jnp.concatenate(turned, axis=1)
+            dq_parts.append(all_turned[0:64])
+            x_parts.append(all_turned[64:128])
+            y_parts.append(all_turned[128:192])
+            dv_parts.append(dv_e)
+            dk_parts.append(dk_e)
+            rolled = pltpu.roll(split_left(flip, acc[...]), 0, 1, stride=1, stride_axis=0)
+            ggv[h, 0:1, :] = jnp.sum(rolled, axis=0, keepdims=True)
+        low = half_lane
+        cols = pl.ds(local * 128, 128)
+        dq[:, cols] = jnp.concatenate(dq_parts, axis=0).T.astype(bf16)
+        dk[:, cols] = jnp.where(low, dk_parts[0], dk_parts[1]).astype(bf16)
+        dv[:, cols] = jnp.where(low, dv_parts[0], dv_parts[1]).astype(bf16)
+        for parts, hots, dest in ((x_parts, hx, ggx), (y_parts, hq2, ggy)):
+            table_grad = dot(jnp.concatenate(parts, axis=0).astype(bf16), hots[...])
+            table_grad = jnp.where(sq_lane < 64, table_grad, 0.0)
+            rolled = pltpu.roll(split_left(flip_halves, table_grad), 0, 1, stride=1, stride_axis=0)
+            dest[2 * p, 0:1, :] = jnp.sum(rolled[0:64], axis=0, keepdims=True)
+            dest[2 * p + 1, 0:1, :] = jnp.sum(rolled[64:128], axis=0, keepdims=True)
+
+    def backward_heads(j, carry):
+        for i in range(2):
+            backward_pair(2 * j + i, i)
+        gn[...] += (
+            dot_nt(dq[...], tile_of(3 * j))
+            + dot_nt(dk[...], tile_of(3 * j + 1))
+            + dot_nt(dv[...], tile_of(3 * j + 2))
+        )
+        ag_sent(j)
+        for i, part in enumerate((dq, dk, dv)):
+            w[3 * j + i] = dot(n1t[...], part[...]).astype(bf16).reshape(shape)
+        rs_tick(ff_groups + OUT_GROUPS + j)
+        return carry
+
+    lax.fori_loop(0, QKV_GROUPS, backward_heads, 0)
+    rs_tick(groups)
+
+    def norm_one_back(i, carry):
+        at = pl.ds(pl.multiple_of(i * 128, 128), 128)
+        stream = tok[at, :].astype(f32)
+        scale = lax.rsqrt(jnp.mean(stream * stream, axis=-1, keepdims=True) + norm_eps)
+        got = gn[at, :]
+        gsum[0] += jnp.sum((got * stream * scale).reshape(16, 8, width), axis=0)
+        scaled = gains[0] * got
+        inner = jnp.mean(scaled * stream, axis=-1, keepdims=True)
+        gtok_ref[at, :] = (
+            grad_res[at, :] + scale * scaled - stream * (scale * scale * scale * inner)
+        )
+        return carry
+
+    lax.fori_loop(0, tok_count // 128, norm_one_back, 0)
+
+    def unhot(bucket_col, count):
+        return (bucket_col == iota((count, 128), 1)).astype(f32).astype(bf16)
+
+    def head_rows(ref, start=0):
+        return jnp.concatenate([ref[h, 0:1, :] for h in range(start, HEADS, 1)], axis=0)
+
+    col_span = iota((span, 128), 0)
+    rel_source = lax.rem(col_span - 127 + span, span)
+    rel_sum = split_dot(head_rows(ggv), unhot(rel_bucket(tok_count - rel_source), span))
+    col_square = iota((128, 128), 0)
+    low_source = lax.rem(col_square - 63 + 128, 128)
+    high_source = lax.rem(col_square - 127 + 128, 128)
+
+    def signed(source):
+        return jnp.where(source < 64, source, source - 128)
+
+    low_hot = unhot(layout_bucket(-signed(low_source)), 128)
+    high_hot = unhot(layout_bucket(-signed(high_source)), 128)
+    odd = lax.rem(iota((HEADS, 128), 0), 2) == 1
+
+    def layout_sum(ref):
+        lines = head_rows(ref)
+        return jnp.where(odd, split_dot(lines, high_hot), split_dot(lines, low_hot))
+
+    spread = (iota((128, 512), 0) == iota((128, 512), 1) // HEADS).astype(f32).astype(bf16)
+    keep = lax.rem(iota((HEADS, 512), 1), HEADS) == iota((HEADS, 512), 0)
+
+    def flat_table(value):
+        high = value.astype(bf16)
+        rest = (value - high.astype(f32)).astype(bf16)
+        rest_two = (value - high.astype(f32) - rest.astype(f32)).astype(bf16)
+        wide = dot(high, spread) + dot(rest, spread) + dot(rest_two, spread)
+        return jnp.sum(jnp.where(keep, wide, 0.0), axis=0, keepdims=True)
+
+    tiles = []
+    for k in range(2):
+        line = jnp.sum(gsum[k], axis=0, keepdims=True)
+        tiles += [line[:, 128 * n : 128 * (n + 1)] for n in range(width // 128)]
+    for value in (rel_sum, layout_sum(ggx), layout_sum(ggy)):
+        line = flat_table(value)
+        tiles += [line[:, 128 * n : 128 * (n + 1)] for n in range(4)]
+    for d in range(len(devs)):
+        line = jnp.zeros((1, 128), f32)
+        for n in range(d * per // 128, (d * per + per - 1) // 128 + 1):
+            shift = 128 * n - d * per
+            moved = pltpu.roll(tiles[n], shift % 128, 1)
+            inside = jnp.logical_and(lane1 >= shift, lane1 < min(shift + 128, per))
+            line = jnp.where(inside, moved, line)
+        sga[d : d + 1, :] = line
+
+    def exchange(k, mine, landed, dev):
+        copy = remote(mine, landed, sm_send.at[4 + k], sm_recv.at[4 + k], dev)
+        copy.start()
+        copy.wait_send()
+        copy.wait_recv()
+
+    def sum_all(k, mine, landed, lined):
+        for i, dev in enumerate((sib, xnb, ynb)):
+            exchange(k + i, mine, landed.at[i], dev)
+            mine[...] = mine[...] + landed[i]
+        lined[z] = mine[...]
+        for i in range(1, nz):
+            remote(lined.at[z], lined.at[z], sm_send.at[k + 7], sm_recv.at[k + 7], zdev(i)).start()
+        three = lined.at[pl.ds(0, nz - 1)]
+        copy = remote(three, three, sm_send.at[k + 7], sm_recv.at[k + 7], zdev(1))
+        copy.wait_send()
+        copy.wait_recv()
+        total = lined[0]
+        for i in range(1, nz):
+            total = total + lined[i]
+        return total
+
+    small_total = sum_all(0, sga, sgr, sgz)
+    me = ((y * 2 + c) * nz + z) * nx + x
+    mine = iota(small_total.shape, 0) == me
+    osmall_ref[...] = jnp.sum(jnp.where(mine, small_total, 0.0), axis=0, keepdims=True)
+    for n in range(groups + 1, groups + 4):
+        rs_tick(n)
+
+    squares = jnp.zeros((8, TILE), f32)
+    for t in range(own.shape[0]):
+        value = own[t]
+        squares = squares + jnp.sum((value * value).reshape(rows // 8, 8, TILE), axis=0)
+    nbr[3] = squares[:, 0:128] + squares[:, 128:256]
+    all_squares = sum_all(4, nbr.at[3], nbr, nbz)
+    total = jnp.sum(all_squares) + jnp.sum(small_total * small_total)
+    norm_ref[...] = jnp.full((8, 128), 1.0, f32) * total
+    for j in range(QKV_GROUPS):
+        cols = pl.ds(j * TILE, TILE)
+        for i in range(3):
+            oattn_ref[i, :, cols] = own[3 * j + i]
+        oattn_ref[3, :, cols] = own[OUT_START + j]
+    for f in range(ff_groups):
+        cols = pl.ds(f * TILE, TILE)
+        for i in range(2):
+            oin_ref[i, :, cols] = own[FF_START + 3 * f + i]
+        odown_ref[:, cols] = own[FF_START + 3 * f + 2]
+    for g in range(groups):
+        rs_sent(g)
+
+
+def fused_on_device(
+    tokens,
+    cotangent,
+    page_lengths,
+    layout_pos,
+    attn_master,
+    attn_first,
+    attn_second,
+    ffin_master,
+    ffin_first,
+    ffin_second,
+    down_master,
+    down_first,
+    down_second,
+    small_master,
+    small_first,
+    small_second,
+    *,
+    ny,
+    nz,
+    nx,
+):
+    f32, bf16 = jnp.float32, jnp.bfloat16
+    tok_count, width = tokens.shape
+    rows, ff = down_master.shape
+    per = small_master.shape[0]
+    ff_groups = ff // TILE
+    tiles = FF_START + 3 * ff_groups
+    groups = QKV_GROUPS + OUT_GROUPS + ff_groups
+    pairs = HEADS // 2
+    vmem, dma = pltpu.VMEM, pltpu.SemaphoreType.DMA
+    square = (tok_count, width)
+    scratch = [
+        vmem((tiles, ny, 2, nz, nx, rows, TILE), bf16),
+        vmem((SLOTS, 3, ny, nz, nx, rows, TILE), bf16),
+        vmem((SLOTS, 2, 3, nz, HALF, TILE), bf16),
+        vmem((SLOTS, 2, 3, nz, rows, TILE), bf16),
+        vmem((SLOTS, nz - 1, 3, rows, TILE), bf16),
+        vmem((tiles, rows, TILE), f32),
+        vmem((ny, 2, nz, nx, 8, 128), f32),
+        vmem((ny * 2 * nz * nx, 128), f32),
+        vmem((3, ny * 2 * nz * nx, 128), f32),
+        vmem((nz, ny * 2 * nz * nx, 128), f32),
+        vmem((4, 8, 128), f32),
+        vmem((nz, 8, 128), f32),
+        vmem(square, bf16),
+        vmem(square, bf16),
+        vmem((width, tok_count), bf16),
+        vmem((pairs, tok_count, 128), bf16),
+        vmem((pairs, tok_count, 128), bf16),
+        vmem((pairs, tok_count, 128), bf16),
+        vmem(square, bf16),
+        vmem((width, tok_count), bf16),
+        vmem(square, f32),
+        vmem(square, bf16),
+        vmem((width, tok_count), bf16),
+        vmem(square, bf16),
+        vmem((width, tok_count), bf16),
+        vmem(square, f32),
+        vmem(square, bf16),
+        vmem((pairs, 128, 128), bf16),
+        vmem((HEADS, 128, 128), bf16),
+        vmem((HEADS, 8, 2 * tok_count), f32),
+        vmem((HEADS, 8, tok_count), f32),
+        vmem((HEADS, 8, 2 * tok_count), f32),
+        vmem((HEADS, 8, 128), f32),
+        vmem((HEADS, 8, 128), f32),
+        vmem((128, 2 * tok_count), f32),
+        vmem((tok_count, 128), bf16),
+        vmem((tok_count, 128), bf16),
+        vmem((tok_count, 128), bf16),
+        vmem((tok_count, 128), bf16),
+        vmem((64, tok_count), bf16),
+        vmem((64, tok_count), bf16),
+        vmem((tok_count, TILE), bf16),
+        vmem((tok_count, TILE), bf16),
+        vmem((tok_count, TILE), bf16),
+        vmem((2, 1, width), f32),
+        vmem((2, 8, width), f32),
+        dma((groups,)),
+        dma((2,)),
+        dma((6, groups)),
+        dma((6, groups)),
+        dma((6, groups)),
+        dma((6, groups)),
+        dma((12,)),
+        dma((12,)),
+    ]
+    in_vmem = pl.BlockSpec(memory_space=pltpu.VMEM)
+    in_hbm = pl.BlockSpec(memory_space=pl.ANY)
+    weights = attn_master.size + ffin_master.size + down_master.size
+    block_out, grad_tokens, owned_attn, owned_in, owned_down, owned_small, squares = pl.pallas_call(
+        functools.partial(layer_kernel, (ny, nz, nx, per, ff_groups)),
+        out_shape=[
+            jax.ShapeDtypeStruct(square, bf16),
+            jax.ShapeDtypeStruct(square, f32),
+            jax.ShapeDtypeStruct(attn_master.shape, f32),
+            jax.ShapeDtypeStruct(ffin_master.shape, f32),
+            jax.ShapeDtypeStruct(down_master.shape, f32),
+            jax.ShapeDtypeStruct((1, 128), f32),
+            jax.ShapeDtypeStruct((8, 128), f32),
+        ],
+        in_specs=[pl.BlockSpec(memory_space=pltpu.SMEM), in_vmem, in_vmem] + [in_hbm] * 5,
+        out_specs=[in_vmem] * 7,
+        scratch_shapes=scratch,
+        compiler_params=pltpu.CompilerParams(
+            collective_id=0, has_side_effects=True, vmem_limit_bytes=VMEM_BYTES
+        ),
+        cost_estimate=pl.CostEstimate(
+            flops=6 * tok_count * weights * ny * 2 * nz * nx,
+            bytes_accessed=24 * weights,
+            transcendentals=3 * tok_count * tok_count * HEADS,
+        ),
+    )(
+        page_lengths,
+        layout_pos,
+        small_master.reshape(1, per),
+        tokens,
+        cotangent,
+        attn_master,
+        ffin_master,
+        down_master,
+    )
+    grad_norm = jnp.sqrt(squares[0, 0])
+    clip_scale = clip_max / jnp.maximum(grad_norm, clip_max)
+    attn_new = adamw_update(
+        attn_master, attn_first, attn_second, owned_attn * clip_scale, matrix_rate, decay_rate
+    )
+    ffin_new = adamw_update(
+        ffin_master, ffin_first, ffin_second, owned_in * clip_scale, matrix_rate, decay_rate
+    )
+    down_new = adamw_update(
+        down_master, down_first, down_second, owned_down * clip_scale, matrix_rate, decay_rate
+    )
+    small_new = adamw_update(
+        small_master, small_first, small_second, owned_small[0, :per] * clip_scale, small_rate, 0.0
+    )
+    return (
+        block_out,
+        grad_tokens,
+        grad_norm,
+        attn_new[0],
+        attn_new[1],
+        attn_new[2][1:],
+        attn_new[2][0],
+        ffin_new[0],
+        ffin_new[1],
+        ffin_new[2],
+        down_new[0],
+        down_new[1],
+        down_new[2],
+        small_new[0],
+        small_new[1],
+        small_new[2],
+    )
+
+
+def choose(mesh, width):
+    n_dp, n_fsdp = mesh.shape["dp"], mesh.shape["fsdp"]
+    rows = width // (n_dp * n_fsdp)
+    if n_dp == 4 and n_fsdp % 2 == 0 and rows % (2 * HALF) == 0:
+        return functools.partial(fused_on_device, ny=n_dp // 2, nz=n_fsdp // 2, nx=2)
+    return on_device
+
+
+def sharded(mesh, program):
     return jax.shard_map(
-        on_device,
+        program,
         mesh=mesh,
         in_specs=(
             P(("dp", "fsdp"), None),
@@ -342,3 +1416,10 @@
         ),
         check_vma=False,
     )
+
+
+def solution(mesh):
+    def step(*args):
+        return sharded(mesh, choose(mesh, args[0].shape[1]))(*args)
+
+    return step

time: 1320 us -> 289 us (0.22)
  waiting for transfers between devices: 797 us -> 0 us
  Pallas kernels: 0 us -> 274 us
  matrix products: 197 us -> 0 us
  blocking collectives: 123 us -> 0 us
  local copies, waits for them, and re-layouts: 129 us -> 6.28 us
  other arithmetic: 44.3 us -> 6.32 us
  between operations: 20.4 us -> 2.66 us
    unnamed x6 -> x0, waiting for transfers between devices: 475 us -> none
    pallas_call x0 -> x1, Pallas kernels: none -> 274 us  [fused_on_device(): pl.pallas_call(functools.partial(layer_kernel, (ny, nz, nx, per, ff_group...]
    reduce_scatter x1 -> x0, waiting for transfers between devices: 246 us -> none  [on_device(): lax.psum_scatter(grad_down, ('dp', 'fsdp'), scatter_dimension=0, tiled=True)]
    dot_general x24 -> x0, matrix products: 176 us -> none  [the longest x1 19 us: block_scores(): jnp.einsum('ihe,jhe->hij', query_rows, key_rows, preferred_element_type=f32)]
    unnamed x2 -> x0, blocking collectives: 84.1 us -> none
    all_gather x3 -> x0, waiting for transfers between devices: 75.5 us -> none  [the longest x1 56.6 us: on_device(): lax.all_gather(down_low, ('dp', 'fsdp'), axis=0, tiled=True)]
    psum x1 -> x0, blocking collectives: 39.3 us -> none  [on_device(): grad_norm = jnp.sqrt(lax.psum(local_squares, ('dp', 'fsdp')))]
    unnamed x68 -> x33, local copies, waits for them, and re-layouts: 39.4 us -> 3.66 us
  transfers between devices with their start and end apart: 5 -> 0, of which waited for: 4 -> 0; matrix products, arithmetic and copies ran while one was open for 14% -> 0% of each run, Pallas kernels for 0% -> 0%
where the time goes in v1:
time: 289 us
  Pallas kernels  274 us (95%)
  other arithmetic  6.32 us (2%)
  local copies, waits for them, and re-layouts  6.28 us (2%)
    pallas_call x1, Pallas kernels, fused_on_device(): pl.pallas_call(functools.partial(layer_kernel, (ny, nz, nx, per, ff_group...  274 us
    sub x4, other arithmetic, adamw_update(): master - step_rate * (first_hat / (jnp.sqrt(second_hat) + adam_eps) + wei...  6.32 us

profile of v1, /device:TPU:0, one launch (start us, length us, event | category | flops | bytes accessed | tf_op | source)
XLA Modules:
  0.0 289.2 jit_solution(5753776217635634094)
XLA Ops:
  0.6 1.3 copy.32.page_ref
  1.9 273.9 %shard_map.279 = (bf16[512,1024]{1,0:T(8,128)(2,1)}, f32[512,1024]{1,0:T(8,128)}, f32[4,32,1024]{2,1,0:T(8,128)}, f32[2,32,2816]{2,1,0:T(8,128)}, f32[32,2816]{1...) custom-call(s32[2,1]{1,0:T(2,128)} %copy.32.page_ref, s32[2,512]{1,0:T(2,128)} %pos_ref.1, f32[1,112]{1,0:T(1,128)} %bitcast.9, ...), custom_call_target="tpu_custom_call" | custom-call | flops 39460012032 | bytes 9633792 | tf_op jit(solution)/shard_map/pallas_call | solution.py:1303
  275.9 1.2 slice.12
  277.8 0.0 copy-done.6
  277.8 0.0 copy-start.2
  277.8 0.0 copy-start.3
  277.8 0.0 copy-start.4
  277.8 0.0 copy-start.5
  277.8 2.9 multiply_subtract_fusion.1
  280.7 0.8 slice.16
  281.5 0.7 slice_bitcast_fusion
  282.1 0.0 copy-done.2
  282.1 0.0 copy-done.3
  282.1 0.0 copy-done.4
  282.1 0.0 copy-done.5
  282.1 0.0 copy-start.7
  282.2 0.0 copy-start.8
  282.2 0.0 copy-start.9
  282.2 0.0 copy-start.10
  282.2 1.7 multiply_subtract_fusion
  283.9 0.0 copy-start.1
  284.0 0.0 copy-done.7
  284.0 0.0 copy-done.8
  284.0 0.0 copy-done.9
  284.0 0.0 copy-done.10
  284.0 1.2 multiply_subtract_fusion.2
  285.2 0.0 copy-done.11
  285.2 0.0 copy-done.13
  285.2 0.5 multiply_subtract_fusion.3
  285.7 1.0 copy.35
  286.7 0.0 copy-done
  286.7 1.3 copy.36
  (9 shorter events, 0.0 us)
Async XLA Ops:
  1.9 275.8 %copy-start.6 = (f32[4,32,1024]{2,1,0:T(8,128)S(1)}, f32[4,32,1024]{2,1,0:T(8,128)}, u32[]{:S(2)}) copy-start(f32[4,32,1024]{2,1,0:T(8,128)} %attn_hbm.1) | copy-start | bytes 1572868
  277.8 4.3 %copy-start.2 = (f32[2,32,2816]{2,1,0:T(8,128)S(1)}, f32[2,32,2816]{2,1,0:T(8,128)}, u32[]{:S(2)}) copy-start(f32[2,32,2816]{2,1,0:T(8,128)} %ffin_hbm.1) | copy-start | bytes 2162692
  277.8 4.3 %copy-start.3 = (f32[2,32,2816]{2,1,0:T(8,128)S(1)}, f32[2,32,2816]{2,1,0:T(8,128)}, u32[]{:S(2)}) copy-start(f32[2,32,2816]{2,1,0:T(8,128)} %param.24) | copy-start | bytes 2162692
  277.8 4.3 %copy-start.4 = (f32[2,32,2816]{2,1,0:T(8,128)S(1)}, f32[2,32,2816]{2,1,0:T(8,128)}, u32[]{:S(2)}) copy-start(f32[2,32,2816]{2,1,0:T(8,128)} %param.25) | copy-start | bytes 2162692
  277.8 4.3 %copy-start.5 = (f32[2,32,2816]{2,1,0:T(8,128)S(1)}, f32[2,32,2816]{2,1,0:T(8,128)}, u32[]{:S(2)}) copy-start(f32[2,32,2816]{2,1,0:T(8,128)} %get-tuple-element.27) | copy-start | bytes 2162692
  282.1 1.8 copy-start.7
  282.2 1.8 copy-start.8
  282.2 1.8 copy-start.9
  282.2 1.8 copy-start.10
  283.9 1.3 copy-start.11
  283.9 1.3 copy-start.12
  283.9 1.3 copy-start.13
  283.9 1.3 copy-start.14
  283.9 1.8 copy-start.1
  284.0 2.7 copy-start

commit v2 on v1

--- a/solution.py
+++ b/solution.py
@@ -309,6 +309,17 @@
 HALF = 16
 SLOTS = 4
 VMEM_BYTES = 63 * 2**20
+Z_SLOTS = 10
+AHEAD = 3
+LATE_GROUPS = 3
+SUM_LAG = 5
+Z_FIRST_SUMS = (1, 5, 9)
+LAGS = (1, 2, 3, 5, 7)
+LINE_LAG = 2
+D_SLOTS = 4
+VMEM_BYTES = 63 * 2**20
+FIRST_AHEAD = 0
+LINE = 4
 QKV_GROUPS = 4
 OUT_GROUPS = 2
 OUT_START = 12
@@ -348,11 +359,9 @@
     attn_hbm,
     ffin_hbm,
     down_hbm,
-    out_ref,
+    out_hbm,
     gtok_ref,
-    oattn_ref,
-    oin_ref,
-    odown_ref,
+    own,
     osmall_ref,
     norm_ref,
     w,
@@ -360,9 +369,10 @@
     rd,
     re,
     rf,
-    own,
+    rbz,
+    rbd,
+    rbe,
     smb,
-    sga,
     sgr,
     sgz,
     nbr,
@@ -381,12 +391,10 @@
     gout,
     goutt,
     gn,
-    gctx,
     kxs,
     km,
     gv,
     lse,
-    ggv,
     ggx,
     ggy,
     acc,
@@ -405,6 +413,10 @@
     in_sem,
     ag_send,
     ag_recv,
+    late_send,
+    late_recv,
+    bl_send,
+    bl_recv,
     rs_send,
     rs_recv,
     sm_send,
@@ -426,13 +438,32 @@
     def zdev(k):
         return device(y, c, lax.rem(z + k, nz), x)
 
+    inner = jnp.logical_and(z > 0, z < LINE - 1)
+    across = lax.rem(z + 2, LINE)
+    edge = jnp.where(z < 2, 0, LINE - 1)
+    inward = jnp.where(z < 2, 1, LINE - 2)
+    far_end = LINE - 1 - edge
+    dev_up, dev_down = device(y, c, jnp.minimum(z + 1, LINE - 1), x), device(y, c, jnp.maximum(z - 1, 0), x)
+    dev_across, dev_edge, dev_inward = (device(y, c, at, x) for at in (across, edge, inward))
+
+    def to_sides(send_up, send_down):
+        pl.when(z < LINE - 1)(send_up)
+        pl.when(z > 0)(send_down)
+
     def remote(src, dst, send, recv, dev):
         return pltpu.make_async_remote_copy(
             src_ref=src, dst_ref=dst, send_sem=send, recv_sem=recv, device_id=dev, device_id_type=MESH
         )
 
+    cube = [(a, b, d) for a in range(ny) for b in range(2) for d in range(nx)][1:]
+
+    def cube_dev(step):
+        return device(*(1 - at if turn else at for at, turn in zip((y, c), step)), z, 1 - x if step[2] else x)
+
+    near = (y * 2 + c) * nx + x
+
     barrier = pltpu.get_barrier_semaphore()
-    for dev in [sib, xnb, ynb] + [zdev(k) for k in range(1, nz)]:
+    for dev in [cube_dev(step) for step in cube] + [zdev(k) for k in range(1, nz)]:
         pl.semaphore_signal(barrier, inc=1, device_id=dev, device_id_type=MESH)
 
     def on_group(g, fn):
@@ -496,26 +527,138 @@
         t = pl.ds(t0, count)
         return t, (lambda i: ag_send.at[i, g]), (lambda i: ag_recv.at[i, g])
 
+    late_start = groups - LATE_GROUPS
+
+    def on_early(g, fn):
+        if isinstance(g, int):
+            if g < late_start:
+                on_group(g, fn)
+        else:
+            on_group(jnp.where(g < late_start, g, -1), fn)
+
+    def on_late(g, fn):
+        if isinstance(g, int):
+            if late_start <= g < groups:
+                on_group(g, fn)
+        else:
+
+            @pl.when(jnp.logical_and(g >= late_start, g < groups))
+            def _():
+                fn(FF_START + 3 * (g - QKV_GROUPS - OUT_GROUPS), 3, g)
+
+    def late1(g):
+        def go(t0, count, g):
+            t, s, r = ag_parts(t0, count, g)
+            mine = w.at[t, y, c, z, x]
+            remote(mine, mine, s(1), r(1), xnb).start()
+            remote(mine, mine, s(2), r(2), ynb).start()
+
+        on_late(g, go)
+
+    def late2(g):
+        def go(t0, count, g):
+            t, s, r = ag_parts(t0, count, g)
+            xpart = w.at[t, y, c, z, 1 - x]
+            ypart = w.at[t, 1 - y, c, z, x]
+            remote(xpart, xpart, s(1), r(1), xnb).wait_recv()
+            remote(ypart, ypart, s(2), r(2), ynb).wait_recv()
+            xhalf = w.at[t, y, c, z, 1 - x, pl.ds(0, HALF)]
+            yhalf = w.at[t, 1 - y, c, z, x, pl.ds(HALF, HALF)]
+            remote(xhalf, xhalf, s(4), r(4), ynb).start()
+            remote(yhalf, yhalf, s(3), r(3), xnb).start()
+
+        on_late(g, go)
+
+    def late3(g):
+        def go(t0, count, g):
+            t, s, r = ag_parts(t0, count, g)
+            low = w.at[t, 1 - y, c, z, 1 - x, pl.ds(0, HALF)]
+            high = w.at[t, 1 - y, c, z, 1 - x, pl.ds(HALF, HALF)]
+            remote(low, low, s(4), r(4), ynb).wait_recv()
+            remote(high, high, s(3), r(3), xnb).wait_recv()
+
+        on_late(g, go)
+
+    def late_tile(b):
+        return FF_START + 3 * (ff_groups - LATE_GROUPS) + b
+
+    def late_line(b):
+        square = w.at[late_tile(b), :, c, z]
+        s, r = late_send, late_recv
+        to_sides(
+            lambda: remote(square, square, s.at[0, b], r.at[0, b], dev_up).start(),
+            lambda: remote(square, square, s.at[0, b], r.at[0, b], dev_down).start(),
+        )
+        remote(square, square, s.at[1, b], r.at[1, b], dev_across).start()
+
+    def late_relay(b):
+        landed = w.at[late_tile(b), :, c, across]
+        s, r = late_send, late_recv
+        remote(landed, landed, s.at[1, b], r.at[1, b], dev_across).wait_recv()
+
+        @pl.when(inner)
+        def _():
+            remote(landed, landed, s.at[0, b], r.at[0, b], dev_edge).start()
+
+    def late_step(t, fn):
+        ticks = 3 * LATE_GROUPS * 3 // 2
+        if isinstance(t, int):
+            if 1 <= t <= ticks and t % 3:
+                fn(t - 1 - t // 3)
+        else:
+            inside = jnp.logical_and(jnp.logical_and(t >= 1, t <= ticks), lax.rem(t, 3) != 0)
+
+            @pl.when(inside)
+            def _():
+                fn(t - 1 - t // 3)
+
+    def late4(g):
+        def go(t0, count, g):
+            t, s, r = ag_parts(t0, count, g)
+            for i in range(3):
+                b = t0 + i - late_tile(0)
+                two = w.at[t0 + i, :, c, pl.ds(0, 2)]
+                remote(two, two, late_send.at[0, b], late_recv.at[0, b], dev_across).wait_recv()
+            plane = w.at[t, :, c]
+            remote(plane, plane, s(5), r(5), sib).start()
+
+        on_late(g, go)
+
     def ag1(g):
         def go(t0, count, g):
             t, s, r = ag_parts(t0, count, g)
             mine = w.at[t, y, c, z, x]
-            for k in range(1, nz):
-                remote(mine, mine, s(0), r(0), zdev(k)).start()
-
-        on_group(g, go)
+            to_sides(
+                lambda: remote(mine, mine, s(0), r(0), dev_up).start(),
+                lambda: remote(mine, mine, s(0), r(0), dev_down).start(),
+            )
+            remote(mine, mine, s(6), r(6), dev_across).start()
+
+        on_early(g, go)
+
+    def ag1_relay(g):
+        def go(t0, count, g):
+            t, s, r = ag_parts(t0, count, g)
+            landed = w.at[t, y, c, across, x]
+            remote(landed, landed, s(6), r(6), dev_across).wait_recv()
+
+            @pl.when(inner)
+            def _():
+                remote(landed, landed, s(0), r(0), dev_edge).start()
+
+        on_early(g, go)
 
     def ag2(g):
         def go(t0, count, g):
             t, s, r = ag_parts(t0, count, g)
-            three = w.at[t, y, c, pl.ds(0, nz - 1), x]
-            remote(three, three, s(0), r(0), zdev(1)).wait_recv()
+            two = w.at[t, y, c, pl.ds(0, 2), x]
+            remote(two, two, s(0), r(0), dev_across).wait_recv()
             column = w.at[t, y, c, :, x]
             remote(column, column, s(1), r(1), xnb).start()
             remote(column, column, s(2), r(2), ynb).start()
             remote(column, column, s(5), r(5), sib).start()
 
-        on_group(g, go)
+        on_early(g, go)
 
     def ag3(g):
         def go(t0, count, g):
@@ -531,7 +674,7 @@
             remote(yhalf, yhalf, s(3), r(3), xnb).start()
             remote(ycol, ycol, s(5), r(5), sib).start()
 
-        on_group(g, go)
+        on_early(g, go)
 
     def ag4(g):
         def go(t0, count, g):
@@ -543,7 +686,7 @@
             diag = w.at[t, 1 - y, c, :, 1 - x]
             remote(diag, diag, s(5), r(5), sib).start()
 
-        on_group(g, go)
+        on_early(g, go)
 
     def ag5(g):
         def go(t0, count, g):
@@ -556,23 +699,51 @@
     def ag_sent(g):
         def go(t0, count, g):
             t, s, r = ag_parts(t0, count, g)
-            three = w.at[t, y, c, pl.ds(0, nz - 1), x]
+            one = w.at[t, y, c, z, x]
             column = w.at[t, y, c, :, x]
             half = w.at[t, y, c, :, x, pl.ds(0, HALF)]
             plane = w.at[t, :, c]
-            remote(three, three, s(0), r(0), zdev(1)).wait_send()
-            remote(column, column, s(1), r(1), xnb).wait_send()
-            remote(column, column, s(2), r(2), ynb).wait_send()
-            remote(half, half, s(3), r(3), xnb).wait_send()
-            remote(half, half, s(4), r(4), ynb).wait_send()
-            remote(plane, plane, s(5), r(5), sib).wait_send()
-
-        on_group(g, go)
+            for i, part in ((1, column), (2, column), (3, half), (4, half), (5, plane), (6, one)):
+                remote(part, part, s(i), r(i), sib).wait_send()
+            sent_sides(w.at[t, y, c, pl.ds(0, 3), x], one, s(0), r(0))
+
+        on_early(g, go)
+
+        def go_late(t0, count, g):
+            t, s, r = ag_parts(t0, count, g)
+            one = w.at[t, y, c, z, x]
+            half = w.at[t, y, c, z, x, pl.ds(0, HALF)]
+            plane = w.at[t, :, c]
+            for i, part in ((1, one), (2, one), (3, half), (4, half), (5, plane)):
+                remote(part, part, s(i), r(i), sib).wait_send()
+            for i in range(3):
+                b = t0 + i - late_tile(0)
+                square = w.at[t0 + i, :, c, z]
+                remote(square, square, late_send.at[1, b], late_recv.at[1, b], sib).wait_send()
+                sent_sides(
+                    w.at[t0 + i, :, c, pl.ds(0, 3)], square, late_send.at[0, b], late_recv.at[0, b]
+                )
+
+        on_late(g, go_late)
+
+    def sent_sides(three, one, s, r):
+        @pl.when(inner)
+        def _():
+            remote(three, three, s, r, sib).wait_send()
+
+        @pl.when(jnp.logical_not(inner))
+        def _():
+            remote(one, one, s, r, sib).wait_send()
 
     def ag_tick(t):
-        ag2(t)
+        ag1(t + AHEAD)
+        ag1_relay(t + FIRST_AHEAD + 1)
+        ag2(t + FIRST_AHEAD)
+        late_step(t, late_line)
         ag3(t - 1)
+        late_step(t - 3, late_relay)
         ag4(t - 2)
+        late4(t - 2)
         ag5(t - 3)
 
     def rs_group(n):
@@ -591,16 +762,43 @@
         )
         return jnp.where(jnp.logical_or(n < 0, n >= groups), -1, g)
 
-    def on_sum(n, fn):
-        slot = n % SLOTS if isinstance(n, int) else lax.rem(n + SLOTS, SLOTS)
+    def z_first(n):
+        if isinstance(n, int):
+            return n in Z_FIRST_SUMS
+        return functools.reduce(jnp.logical_or, [n == m for m in Z_FIRST_SUMS])
+
+    def on_sum(n, fn, kind=None):
+        which = z_first(n)
+        if isinstance(n, int):
+            if kind is not None and which != kind:
+                return
+            slots = (n % SLOTS, n % Z_SLOTS, sum(n > m for m in Z_FIRST_SUMS), n % D_SLOTS)
+            g = rs_group(n)
+        else:
+            bank = sum((n > m).astype(jnp.int32) for m in Z_FIRST_SUMS)
+            slots = tuple(lax.rem(n + 10 * k, k) for k in (SLOTS, Z_SLOTS)) + (bank, lax.rem(n + 10 * D_SLOTS, D_SLOTS))
+            g = rs_group(n)
+            if kind is not None:
+                g = jnp.where(which if kind else jnp.logical_not(which), g, -1)
 
         def go(t0, count, g):
-            fn(t0, count, slot, (lambda i: rs_send.at[i, g]), (lambda i: rs_recv.at[i, g]))
-
-        on_group(rs_group(n), go)
+            fn(t0, count, slots, (lambda i: rs_send.at[i, g]), (lambda i: rs_recv.at[i, g]))
+
+        if kind:
+            if isinstance(n, int):
+                on_group(g, go)
+            else:
+
+                @pl.when(g >= 0)
+                def _():
+                    go(FF_START + 3 * (g - QKV_GROUPS - OUT_GROUPS), 3, g)
+
+        else:
+            on_group(g, go)
 
     def rs0(n):
-        def go(t0, count, slot, s, r):
+        def go(t0, count, slots, s, r):
+            slot = slots[0]
             remote(
                 w.at[pl.ds(t0, count), :, 1 - c], rh.at[slot, pl.ds(0, count)], s(0), r(0), sib
             ).start()
@@ -608,7 +806,8 @@
         on_sum(n, go)
 
     def rs1(n):
-        def go(t0, count, slot, s, r):
+        def go(t0, count, slots, s, r):
+            slot = slots[0]
             t = pl.ds(t0, count)
             landed = rh.at[slot, pl.ds(0, count)]
             remote(w.at[t, :, 1 - c], landed, s(0), r(0), sib).wait_recv()
@@ -619,19 +818,103 @@
                 return carry
 
             lax.fori_loop(0, count, add, 0)
+
+        on_sum(n, go)
+
+        def go_early(t0, count, slots, s, r):
             for k, dev in ((0, xnb), (1, ynb)):
                 remote(
-                    w.at[t, 1 - y, c, :, 1 - x, pl.ds(k * HALF, HALF)],
-                    rd.at[slot, k, pl.ds(0, count)],
+                    w.at[pl.ds(t0, count), 1 - y, c, :, 1 - x, pl.ds(k * HALF, HALF)],
+                    rd.at[slots[3], k, pl.ds(0, count)],
                     s(1 + k),
                     r(1 + k),
                     dev,
                 ).start()
 
-        on_sum(n, go)
+        on_sum(n, go_early, False)
+
+    def rs1_line(n, i):
+        def go_line(t0, count, slots, s, r):
+            bank = slots[2]
+            sems = line_sems(bank, i)
+            line_sends(lambda at: w.at[t0 + i, :, c, at], lambda kind: rbz.at[bank, kind, i], *sems)
+
+        on_sum(n, go_line, True)
+
+    def line_sems(bank, i):
+        return (lambda kind: bl_send.at[kind - 5, 3 * bank + i]), (lambda kind: bl_recv.at[kind - 5, 3 * bank + i])
+
+    def line_sends(part, landed, s, r):
+        to_sides(
+            lambda: remote(part(dev_at(z + 1)), landed(0), s(5), r(5), dev_up).start(),
+            lambda: remote(part(dev_at(z - 1)), landed(1), s(6), r(6), dev_down).start(),
+        )
+
+        @pl.when(jnp.logical_not(inner))
+        def _():
+            remote(part(across), landed(2), s(7), r(7), dev_across).start()
+            remote(part(far_end), landed(3), s(8), r(8), dev_inward).start()
+
+    def dev_at(at):
+        return jnp.clip(at, 0, LINE - 1)
+
+    def line_merge(part, landed, s, r, add):
+        @pl.when(inner)
+        def _():
+            remote(part(across), landed(3), s(8), r(8), dev_edge).wait_recv()
+            add()
+            remote(part(across), landed(2), s(7), r(7), dev_across).start()
+
+    def line_wait(part, landed, s, r, add):
+        @pl.when(z > 0)
+        def _():
+            remote(part(z), landed(0), s(5), r(5), dev_down).wait_recv()
+            add(0)
+
+        @pl.when(z < LINE - 1)
+        def _():
+            remote(part(z), landed(1), s(6), r(6), dev_up).wait_recv()
+            add(1)
+
+        remote(part(z), landed(2), s(7), r(7), dev_across).wait_recv()
+        add(2)
+
+    def line_sent(part, s, r):
+        pl.when(z < LINE - 1)(lambda: remote(part, part, s(5), r(5), sib).wait_send())
+        pl.when(z > 0)(lambda: remote(part, part, s(6), r(6), sib).wait_send())
+        remote(part, part, s(7), r(7), sib).wait_send()
+        pl.when(jnp.logical_not(inner))(lambda: remote(part, part, s(8), r(8), sib).wait_send())
+
+    def rs_merge(n):
+        def go(t0, count, slots, s, r):
+            t = pl.ds(t0, count)
+
+            def add():
+                for i in range(count):
+                    w[t0 + i, y, c, across, x] = w[t0 + i, y, c, across, x] + rf[slots[1], 3, i]
+
+            line_merge(
+                lambda at: w.at[t, y, c, at, x], lambda kind: rf.at[slots[1], kind, pl.ds(0, count)], s, r, add
+            )
+
+        on_sum(n, go, False)
+
+    def rs_line_merge(n, i):
+        def go(t0, count, slots, s, r):
+            bank = slots[2]
+
+            def add():
+                for yy in range(ny):
+                    w[t0 + i, yy, c, across] = w[t0 + i, yy, c, across] + rbz[bank, 3, i, yy]
+
+            sems = line_sems(bank, i)
+            line_merge(lambda at: w.at[t0 + i, :, c, at], lambda kind: rbz.at[bank, kind, i], *sems, add)
+
+        on_sum(n, go, True)
 
     def rs2(n):
-        def go(t0, count, slot, s, r):
+        def go(t0, count, slots, s, r):
+            slot = slots[3]
             t = pl.ds(t0, count)
             for k, dev, yy, xx in ((0, xnb, 1 - y, x), (1, ynb, y, 1 - x)):
                 landed = rd.at[slot, k, pl.ds(0, count)]
@@ -644,10 +927,38 @@
                     w.at[t, yy, c, :, xx], re.at[slot, k, pl.ds(0, count)], s(3 + k), r(3 + k), dev
                 ).start()
 
-        on_sum(n, go)
+        on_sum(n, go, False)
+
+    def rs2_line(n):
+        def go_line(t0, count, slots, s, r):
+            t = pl.ds(t0, count)
+            bank = slots[2]
+            for i in range(count):
+
+                def add(kind, i=i):
+                    for yy in range(ny):
+                        w[t0 + i, yy, c, z] = w[t0 + i, yy, c, z] + rbz[bank, kind, i, yy]
+
+                line_wait(
+                    lambda at, i=i: w.at[t0 + i, :, c, at],
+                    lambda kind, i=i: rbz.at[bank, kind, i],
+                    *line_sems(bank, i),
+                    add,
+                )
+            for k, dev in ((0, xnb), (1, ynb)):
+                remote(
+                    w.at[t, 1 - y, c, z, 1 - x, pl.ds(k * HALF, HALF)],
+                    rbd.at[slots[2], k],
+                    s(1 + k),
+                    r(1 + k),
+                    dev,
+                ).start()
+
+        on_sum(n, go_line, True)
 
     def rs3(n):
-        def go(t0, count, slot, s, r):
+        def go(t0, count, slots, s, r):
+            slot = slots[3]
             t = pl.ds(t0, count)
             for k, dev in ((0, xnb), (1, ynb)):
                 landed = re.at[slot, k, pl.ds(0, count)]
@@ -665,85 +976,125 @@
                         + re[slot, 0, i, zz].astype(f32)
                         + re[slot, 1, i, zz].astype(f32)
                     ).astype(bf16)
-            for k in range(1, nz):
-                remote(
-                    w.at[t, y, c, lax.rem(z + k, nz), x],
-                    rf.at[slot, k - 1, pl.ds(0, count)],
-                    s(5),
-                    r(5),
-                    zdev(k),
-                ).start()
-
-        on_sum(n, go)
+            line_sends(
+                lambda at: w.at[t, y, c, at, x], lambda kind: rf.at[slots[1], kind, pl.ds(0, count)], s, r
+            )
+
+        on_sum(n, go, False)
+
+    def rs3_line(n):
+        def go_line(t0, count, slots, s, r):
+            t = pl.ds(t0, count)
+            for k, dev, yy, xx in ((0, xnb, 1 - y, x), (1, ynb, y, 1 - x)):
+                landed = rbd.at[slots[2], k]
+                rows_k = pl.ds(k * HALF, HALF)
+                remote(w.at[t, 1 - y, c, z, 1 - x, rows_k], landed, s(1 + k), r(1 + k), dev).wait_recv()
+                for i in range(count):
+                    w[t0 + i, yy, c, z, xx, rows_k] = w[t0 + i, yy, c, z, xx, rows_k] + rbd[slots[2], k, i]
+            for k, dev, yy, xx in ((0, xnb, y, 1 - x), (1, ynb, 1 - y, x)):
+                remote(w.at[t, yy, c, z, xx], rbe.at[slots[2], k], s(3 + k), r(3 + k), dev).start()
+
+        on_sum(n, go_line, True)
 
     def rs4(n):
-        def go(t0, count, slot, s, r):
-            landed = rf.at[slot, :, pl.ds(0, count)]
-            remote(landed, landed, s(5), r(5), zdev(1)).wait_recv()
+        def go(t0, count, slots, s, r):
+            t = pl.ds(t0, count)
+
+            def add(kind):
+                for i in range(count):
+                    own[t0 + i] += rf[slots[1], kind, i].astype(f32)
+
+            line_wait(
+                lambda at: w.at[t, y, c, at, x], lambda kind: rf.at[slots[1], kind, pl.ds(0, count)], s, r, add
+            )
+
+        on_sum(n, go, False)
+
+    def rs4_line(n):
+        def go_line(t0, count, slots, s, r):
+            for k, dev in ((0, xnb), (1, ynb)):
+                landed = rbe.at[slots[2], k]
+                remote(landed, landed, s(3 + k), r(3 + k), dev).wait_recv()
             for i in range(count):
-                total = own[t0 + i]
-                for k in range(nz - 1):
-                    total = total + rf[slot, k, i].astype(f32)
-                own[t0 + i] = total
-
-        on_sum(n, go)
-
-    def rs_sent(g):
-        def go(t0, count, g):
+                own[t0 + i] = (
+                    w[t0 + i, y, c, z, x].astype(f32)
+                    + rbe[slots[2], 0, i].astype(f32)
+                    + rbe[slots[2], 1, i].astype(f32)
+                )
+
+        on_sum(n, go_line, True)
+
+    def rs_sent(n):
+        def go(t0, count, slots, s, r):
             t = pl.ds(t0, count)
-            s, r = (lambda i: rs_send.at[i, g]), (lambda i: rs_recv.at[i, g])
             plane = w.at[t, :, c]
             half = w.at[t, y, c, :, x, pl.ds(0, HALF)]
             column = w.at[t, y, c, :, x]
-            three = w.at[t, y, c, pl.ds(0, nz - 1), x]
-            for i, part in enumerate((plane, half, half, column, column, three)):
+            for i, part in enumerate((plane, half, half, column, column)):
                 remote(part, part, s(i), r(i), sib).wait_send()
-
-        on_group(g, go)
+            line_sent(w.at[t, y, c, z, x], s, r)
+
+        on_sum(n, go, False)
+
+        def go_line(t0, count, slots, s, r):
+            t = pl.ds(t0, count)
+            plane = w.at[t, :, c]
+            half = w.at[t, y, c, z, x, pl.ds(0, HALF)]
+            one = w.at[t, y, c, z, x]
+            for i, part in enumerate((plane, half, half, one, one)):
+                remote(part, part, s(i), r(i), sib).wait_send()
+            for i in range(count):
+                line_sent(w.at[t0 + i, :, c, z], *line_sems(slots[2], i))
+
+        on_sum(n, go_line, True)
 
     def rs_tick(n):
         rs0(n)
-        rs1(n - 1)
-        rs2(n - 2)
-        rs3(n - 3)
-        rs4(n - 4)
-
-    sm_steps = (
-        (smb.at[y, c, z, x], None),
-        (smb.at[y, c, :, x], xnb),
-        (smb.at[y, c], ynb),
-        (smb.at[:, c], sib),
-    )
+        rs1(n - LAGS[0])
+        for i in range(3):
+            rs1_line(n - LAGS[0] - i, i)
+        rs2(n - LAGS[1])
+        rs3(n - LAGS[2])
+        for i in range(3):
+            rs_line_merge(n - LAGS[0] - LINE_LAG - i, i)
+        rs_merge(n - LAGS[3])
+        rs4(n - LAGS[4])
+        rs2_line(n - LAGS[0] - 2 * LINE_LAG - 2)
+        rs3_line(n - LAGS[0] - 2 * LINE_LAG - 3)
+        rs4_line(n - LAGS[0] - 2 * LINE_LAG - 4)
+
+    def cast_wait(copy):
+        copy.wait_send()
+        copy.wait_recv()
 
     def sm_start(i):
-        part, dev = sm_steps[i]
         if i == 0:
+            part = smb.at[near, z]
             for k in range(1, nz):
                 remote(part, part, sm_send.at[0], sm_recv.at[0], zdev(k)).start()
         else:
-            remote(part, part, sm_send.at[i], sm_recv.at[i], dev).start()
+            part = smb.at[near]
+            for step in cube:
+                remote(part, part, sm_send.at[1], sm_recv.at[1], cube_dev(step)).start()
 
     def sm_wait(i):
-        part = (
-            smb.at[y, c, pl.ds(0, nz - 1), x],
-            smb.at[y, c, :, 1 - x],
-            smb.at[1 - y, c],
-            smb.at[:, 1 - c],
-        )[i]
-        dev = zdev(1) if i == 0 else sm_steps[i][1]
-        copy = remote(part, part, sm_send.at[i], sm_recv.at[i], dev)
-        copy.wait_recv()
-        copy.wait_send()
-
-    smb[y, c, z, x] = jnp.zeros(smb.shape[4:], f32)
-    smb[y, c, z, x, 0:1, 0:per] = small_ref[...].astype(bf16).astype(f32)
+        part = smb.at[near, pl.ds(0, nz - 1)] if i == 0 else smb.at[pl.ds(0, len(cube))]
+        cast_wait(remote(part, part, sm_send.at[i], sm_recv.at[i], sib))
+
+    smb[near, z] = jnp.zeros(smb.shape[2:], f32)
+    smb[near, z, 0:1, 0:per] = small_ref[...].astype(bf16).astype(f32)
     load_wait(0)
-    pl.semaphore_wait(barrier, 3 + nz - 1)
+    pl.semaphore_wait(barrier, len(cube) + nz - 1)
     sm_start(0)
     ag1(0)
-    for g in range(1, groups):
+    for g in range(1, AHEAD):
         load_wait(g)
         ag1(g)
+    for g in range(late_start, groups):
+        load_wait(g)
+        late1(g)
+    for g in range(AHEAD, late_start):
+        load_wait(g)
 
     lane = iota((tok_count, 128), 1)
     row = iota((tok_count, 128), 0)
@@ -767,7 +1118,13 @@
     hyt[...] = hot_y.T[0:64].astype(bf16)
     sm_wait(0)
     sm_start(1)
+    for g in range(FIRST_AHEAD + 1):
+        ag1_relay(g)
+        if g < FIRST_AHEAD:
+            ag2(g)
     ag_tick(0)
+    for g in range(late_start, groups):
+        late2(g)
     cot_copy.wait()
 
     def mask_out(i, carry):
@@ -779,12 +1136,10 @@
         return carry
 
     lax.fori_loop(0, tok_count // 128, mask_out, 0)
+    for g in range(late_start, groups):
+        late3(g)
+    ag_tick(1)
     sm_wait(1)
-    sm_start(2)
-    ag_tick(1)
-    sm_wait(2)
-    sm_start(3)
-    sm_wait(3)
 
     devs = [(a, b, d, e) for a in range(ny) for b in range(2) for d in range(nz) for e in range(nx)]
     lane1 = iota((1, 128), 1)
@@ -793,7 +1148,8 @@
         tile = jnp.zeros((1, 128), f32)
         for d in range(128 * n // per, (128 * n + 127) // per + 1):
             shift = d * per - 128 * n
-            line = smb[devs[d] + (slice(0, 1), slice(None))]
+            a, b, at_z, at_x = devs[d]
+            line = smb[(a * 2 + b) * nx + at_x, at_z, 0:1, :]
             line = pltpu.roll(line, shift % 128, 1)
             inside = jnp.logical_and(lane1 >= shift, lane1 < shift + per)
             tile = jnp.where(inside, line, tile)
@@ -975,18 +1331,18 @@
         w[t0] = dot(n2t[...], grad_gate).astype(bf16).reshape(shape)
         w[t0 + 1] = dot(n2t[...], grad_up).astype(bf16).reshape(shape)
         w[t0 + 2] = dot(goutt[...], hidden).astype(bf16).reshape(shape)
-        rs_tick(f)
+        rs_tick(f - SUM_LAG)
         return carry
 
     lax.fori_loop(0, ff_groups, feed, 0)
 
     gsum[...] = jnp.zeros_like(gsum)
-    grad_res = mix
+    grad_res, gctx = mix, gout
 
     def norm_two_back(i, carry):
         at = pl.ds(pl.multiple_of(i * 128, 128), 128)
         valid = (iota((128, width), 0) + i * 128 < both_len).astype(f32)
-        out_ref[at, :] = (valid * mix[at, :]).astype(bf16)
+        ctx[at, :] = (valid * mix[at, :]).astype(bf16)
         stream = res[at, :]
         scale = lax.rsqrt(jnp.mean(stream * stream, axis=-1, keepdims=True) + norm_eps)
         got = gn[at, :]
@@ -1000,8 +1356,13 @@
         return carry
 
     lax.fori_loop(0, tok_count // 128, norm_two_back, 0)
+    out_copy = pltpu.make_async_copy(ctx, out_hbm, in_sem.at[0])
+    out_copy.start()
     attended = n2
     shape = w.shape[1:]
+    done = ff_groups - SUM_LAG
+    rs_tick(done)
+    done += 1
     for yy in range(ny):
         for cc in range(2):
             part = jnp.zeros((tok_count, TILE), f32)
@@ -1015,7 +1376,8 @@
             w[OUT_START + e] = (
                 dot(ctxt[...], attended[:, pl.ds(e * TILE, TILE)]).astype(bf16).reshape(shape)
             )
-        rs_tick(ff_groups + i)
+        rs_tick(done)
+        done += 1
 
     flip = (sq_row + sq_lane == 127).astype(f32).astype(bf16)
     flip_halves = jnp.where(
@@ -1063,7 +1425,7 @@
             dv_parts.append(dv_e)
             dk_parts.append(dk_e)
             rolled = pltpu.roll(split_left(flip, acc[...]), 0, 1, stride=1, stride_axis=0)
-            ggv[h, 0:1, :] = jnp.sum(rolled, axis=0, keepdims=True)
+            gv[h, 0:1, :] = jnp.sum(rolled, axis=0, keepdims=True)
         low = half_lane
         cols = pl.ds(local * 128, 128)
         dq[:, cols] = jnp.concatenate(dq_parts, axis=0).T.astype(bf16)
@@ -1077,8 +1439,9 @@
             dest[2 * p + 1, 0:1, :] = jnp.sum(rolled[64:128], axis=0, keepdims=True)
 
     def backward_heads(j, carry):
-        for i in range(2):
-            backward_pair(2 * j + i, i)
+        backward_pair(2 * j, 0)
+        rs_tick(done + 2 * j)
+        backward_pair(2 * j + 1, 1)
         gn[...] += (
             dot_nt(dq[...], tile_of(3 * j))
             + dot_nt(dk[...], tile_of(3 * j + 1))
@@ -1087,11 +1450,12 @@
         ag_sent(j)
         for i, part in enumerate((dq, dk, dv)):
             w[3 * j + i] = dot(n1t[...], part[...]).astype(bf16).reshape(shape)
-        rs_tick(ff_groups + OUT_GROUPS + j)
+        rs_tick(done + 2 * j + 1)
         return carry
 
     lax.fori_loop(0, QKV_GROUPS, backward_heads, 0)
-    rs_tick(groups)
+    done += 2 * QKV_GROUPS
+    rs_tick(done)
 
     def norm_one_back(i, carry):
         at = pl.ds(pl.multiple_of(i * 128, 128), 128)
@@ -1107,6 +1471,7 @@
         return carry
 
     lax.fori_loop(0, tok_count // 128, norm_one_back, 0)
+    rs_tick(done + 1)
 
     def unhot(bucket_col, count):
         return (bucket_col == iota((count, 128), 1)).astype(f32).astype(bf16)
@@ -1116,7 +1481,7 @@
 
     col_span = iota((span, 128), 0)
     rel_source = lax.rem(col_span - 127 + span, span)
-    rel_sum = split_dot(head_rows(ggv), unhot(rel_bucket(tok_count - rel_source), span))
+    rel_sum = split_dot(head_rows(gv), unhot(rel_bucket(tok_count - rel_source), span))
     col_square = iota((128, 128), 0)
     low_source = lax.rem(col_square - 63 + 128, 128)
     high_source = lax.rem(col_square - 127 + 128, 128)
@@ -1156,57 +1521,199 @@
             moved = pltpu.roll(tiles[n], shift % 128, 1)
             inside = jnp.logical_and(lane1 >= shift, lane1 < min(shift + 128, per))
             line = jnp.where(inside, moved, line)
-        sga[d : d + 1, :] = line
-
-    def exchange(k, mine, landed, dev):
-        copy = remote(mine, landed, sm_send.at[4 + k], sm_recv.at[4 + k], dev)
-        copy.start()
-        copy.wait_send()
-        copy.wait_recv()
-
-    def sum_all(k, mine, landed, lined):
-        for i, dev in enumerate((sib, xnb, ynb)):
-            exchange(k + i, mine, landed.at[i], dev)
-            mine[...] = mine[...] + landed[i]
-        lined[z] = mine[...]
+        sgr[near, d : d + 1, :] = line
+
+    def near_start(k, landed):
+        part = landed.at[near]
+        for step in cube:
+            remote(part, part, sm_send.at[k], sm_recv.at[k], cube_dev(step)).start()
+
+    def near_sum(k, landed, lined):
+        part = landed.at[pl.ds(0, len(cube))]
+        cast_wait(remote(part, part, sm_send.at[k], sm_recv.at[k], sib))
+        total = landed[0]
+        for i in range(1, len(cube) + 1):
+            total = total + landed[i]
+        lined[z] = total
         for i in range(1, nz):
-            remote(lined.at[z], lined.at[z], sm_send.at[k + 7], sm_recv.at[k + 7], zdev(i)).start()
-        three = lined.at[pl.ds(0, nz - 1)]
-        copy = remote(three, three, sm_send.at[k + 7], sm_recv.at[k + 7], zdev(1))
-        copy.wait_send()
-        copy.wait_recv()
+            remote(lined.at[z], lined.at[z], sm_send.at[k + 1], sm_recv.at[k + 1], zdev(i)).start()
+
+    def line_sum(k, lined):
+        part = lined.at[pl.ds(0, nz - 1)]
+        cast_wait(remote(part, part, sm_send.at[k + 1], sm_recv.at[k + 1], sib))
         total = lined[0]
         for i in range(1, nz):
             total = total + lined[i]
         return total
 
-    small_total = sum_all(0, sga, sgr, sgz)
+    near_start(2, sgr)
+    rs_tick(done + 2)
+    near_sum(2, sgr, sgz)
+    for n in range(done + 3, groups + LAGS[4]):
+        rs_tick(n)
+    small_total = line_sum(2, sgz)
     me = ((y * 2 + c) * nz + z) * nx + x
     mine = iota(small_total.shape, 0) == me
     osmall_ref[...] = jnp.sum(jnp.where(mine, small_total, 0.0), axis=0, keepdims=True)
-    for n in range(groups + 1, groups + 4):
-        rs_tick(n)
 
     squares = jnp.zeros((8, TILE), f32)
     for t in range(own.shape[0]):
         value = own[t]
         squares = squares + jnp.sum((value * value).reshape(rows // 8, 8, TILE), axis=0)
-    nbr[3] = squares[:, 0:128] + squares[:, 128:256]
-    all_squares = sum_all(4, nbr.at[3], nbr, nbz)
-    total = jnp.sum(all_squares) + jnp.sum(small_total * small_total)
+    nbr[near] = squares[:, 0:128] + squares[:, 128:256]
+    near_start(4, nbr)
+    out_copy.wait()
+    for n in range(groups):
+        rs_sent(n)
+    near_sum(4, nbr, nbz)
+    total = jnp.sum(line_sum(4, nbz)) + jnp.sum(small_total * small_total)
     norm_ref[...] = jnp.full((8, 128), 1.0, f32) * total
+
+
+def update_kernel(
+    sizes,
+    total_ref,
+    small_grad,
+    small_master,
+    small_first,
+    small_second,
+    own_hbm,
+    block_hbm,
+    gtok_hbm,
+    attn_hbm,
+    attn_first_hbm,
+    attn_second_hbm,
+    ffin_hbm,
+    ffin_first_hbm,
+    ffin_second_hbm,
+    down_hbm,
+    down_first_hbm,
+    down_second_hbm,
+    norm_out,
+    small_master_out,
+    small_first_out,
+    small_second_out,
+    block_out,
+    gtok_out,
+    attn_out,
+    attn_first_out,
+    attn_second_out,
+    query_second_out,
+    ffin_out,
+    ffin_first_out,
+    ffin_second_out,
+    down_out,
+    down_first_out,
+    down_second_out,
+    own,
+    attn,
+    ffin,
+    down,
+    block,
+    gtok,
+    in_sem,
+    out_sem,
+    pass_sem,
+):
+    (ff_groups,) = sizes
+    passing = [
+        pltpu.make_async_copy(block_hbm, block, pass_sem.at[0]),
+        pltpu.make_async_copy(gtok_hbm, gtok, pass_sem.at[1]),
+    ]
+    passed = [
+        pltpu.make_async_copy(block, block_out, pass_sem.at[2]),
+        pltpu.make_async_copy(gtok, gtok_out, pass_sem.at[3]),
+    ]
+    first_tiles, other_tiles = pl.ds(0, FF_START), pl.ds(FF_START, 3 * ff_groups)
+    loads = [
+        [pltpu.make_async_copy(own_hbm.at[first_tiles], own.at[first_tiles], in_sem.at[0])],
+        [pltpu.make_async_copy(own_hbm.at[other_tiles], own.at[other_tiles], in_sem.at[1])],
+        [],
+    ]
+    sources = (
+        (attn_hbm, attn_first_hbm, attn_second_hbm),
+        (ffin_hbm, ffin_first_hbm, ffin_second_hbm),
+        (down_hbm, down_first_hbm, down_second_hbm),
+    )
+    state = (attn, ffin, down)
+    for i in range(3):
+        loads[i] += [
+            pltpu.make_async_copy(src, state[i].at[k], in_sem.at[2 + 3 * i + k])
+            for k, src in enumerate(sources[i])
+        ]
+    for part in loads:
+        for copy in part:
+            copy.start()
+    for copy in passing:
+        copy.start()
+    norm = jnp.sqrt(total_ref[0:1, 0:1])
+    norm_out[...] = norm
+    clip = clip_max / jnp.maximum(norm, clip_max)
+    per = small_master.shape[1]
+    results = adamw_update(
+        small_master[...], small_first[...], small_second[...], small_grad[:, 0:per] * clip, small_rate, 0.0
+    )
+    for ref, value in zip((small_master_out, small_first_out, small_second_out), results):
+        ref[...] = value
+
+    def update(ref, at, tile):
+        results = adamw_update(
+            ref[(0,) + at], ref[(1,) + at], ref[(2,) + at], own[tile] * clip, matrix_rate, decay_rate
+        )
+        for k in range(3):
+            ref[(k,) + at] = results[k]
+
+    every = slice(None)
+    stores = []
+
+    def store(i, pairs):
+        for src, dst in pairs:
+            copy = pltpu.make_async_copy(src, dst, out_sem.at[len(stores)])
+            copy.start()
+            stores.append(copy)
+
+    for copy in loads[0]:
+        copy.wait()
     for j in range(QKV_GROUPS):
         cols = pl.ds(j * TILE, TILE)
         for i in range(3):
-            oattn_ref[i, :, cols] = own[3 * j + i]
-        oattn_ref[3, :, cols] = own[OUT_START + j]
-    for f in range(ff_groups):
-        cols = pl.ds(f * TILE, TILE)
+            update(attn, (i, every, cols), 3 * j + i)
+        update(attn, (3, every, cols), OUT_START + j)
+    store(
+        0,
+        [
+            (attn.at[0], attn_out),
+            (attn.at[1], attn_first_out),
+            (attn.at[2, pl.ds(1, 3)], attn_second_out),
+            (attn.at[2, 0], query_second_out),
+        ],
+    )
+    for copy in loads[1]:
+        copy.wait()
+
+    def update_in(f, carry):
+        cols = pl.ds(pl.multiple_of(f * TILE, TILE), TILE)
         for i in range(2):
-            oin_ref[i, :, cols] = own[FF_START + 3 * f + i]
-        odown_ref[:, cols] = own[FF_START + 3 * f + 2]
-    for g in range(groups):
-        rs_sent(g)
+            update(ffin, (i, every, cols), FF_START + 3 * f + i)
+        return carry
+
+    lax.fori_loop(0, ff_groups, update_in, 0)
+    store(1, [(ffin.at[k], ref) for k, ref in enumerate((ffin_out, ffin_first_out, ffin_second_out))])
+    for copy in loads[2]:
+        copy.wait()
+
+    def update_down(f, carry):
+        cols = pl.ds(pl.multiple_of(f * TILE, TILE), TILE)
+        update(down, (every, cols), FF_START + 3 * f + 2)
+        return carry
+
+    lax.fori_loop(0, ff_groups, update_down, 0)
+    store(2, [(down.at[k], ref) for k, ref in enumerate((down_out, down_first_out, down_second_out))])
+    for arrived, copy in zip(passing, passed):
+        arrived.wait()
+        copy.start()
+    for copy in stores + passed:
+        copy.wait()
 
 
 def fused_on_device(
@@ -1241,18 +1748,20 @@
     pairs = HEADS // 2
     vmem, dma = pltpu.VMEM, pltpu.SemaphoreType.DMA
     square = (tok_count, width)
+    banks = len(Z_FIRST_SUMS)
     scratch = [
         vmem((tiles, ny, 2, nz, nx, rows, TILE), bf16),
         vmem((SLOTS, 3, ny, nz, nx, rows, TILE), bf16),
-        vmem((SLOTS, 2, 3, nz, HALF, TILE), bf16),
-        vmem((SLOTS, 2, 3, nz, rows, TILE), bf16),
-        vmem((SLOTS, nz - 1, 3, rows, TILE), bf16),
-        vmem((tiles, rows, TILE), f32),
-        vmem((ny, 2, nz, nx, 8, 128), f32),
-        vmem((ny * 2 * nz * nx, 128), f32),
-        vmem((3, ny * 2 * nz * nx, 128), f32),
+        vmem((D_SLOTS, 2, 3, nz, HALF, TILE), bf16),
+        vmem((D_SLOTS, 2, 3, nz, rows, TILE), bf16),
+        vmem((Z_SLOTS, 4, 3, rows, TILE), bf16),
+        vmem((banks, 4, 3, ny, nx, rows, TILE), bf16),
+        vmem((banks, 2, 3, HALF, TILE), bf16),
+        vmem((banks, 2, 3, rows, TILE), bf16),
+        vmem((ny * 2 * nx, nz, 8, 128), f32),
+        vmem((ny * 2 * nx, ny * 2 * nz * nx, 128), f32),
         vmem((nz, ny * 2 * nz * nx, 128), f32),
-        vmem((4, 8, 128), f32),
+        vmem((ny * 2 * nx, 8, 128), f32),
         vmem((nz, 8, 128), f32),
         vmem(square, bf16),
         vmem(square, bf16),
@@ -1268,12 +1777,10 @@
         vmem(square, bf16),
         vmem((width, tok_count), bf16),
         vmem(square, f32),
-        vmem(square, bf16),
         vmem((pairs, 128, 128), bf16),
         vmem((HEADS, 128, 128), bf16),
         vmem((HEADS, 8, 2 * tok_count), f32),
         vmem((HEADS, 8, tok_count), f32),
-        vmem((HEADS, 8, 2 * tok_count), f32),
         vmem((HEADS, 8, 128), f32),
         vmem((HEADS, 8, 128), f32),
         vmem((128, 2 * tok_count), f32),
@@ -1290,29 +1797,31 @@
         vmem((2, 8, width), f32),
         dma((groups,)),
         dma((2,)),
-        dma((6, groups)),
-        dma((6, groups)),
-        dma((6, groups)),
-        dma((6, groups)),
-        dma((12,)),
-        dma((12,)),
+        dma((7, groups)),
+        dma((7, groups)),
+        dma((2, 3 * LATE_GROUPS)),
+        dma((2, 3 * LATE_GROUPS)),
+        dma((4, 3 * banks)),
+        dma((4, 3 * banks)),
+        dma((9, groups)),
+        dma((9, groups)),
+        dma((6,)),
+        dma((6,)),
     ]
     in_vmem = pl.BlockSpec(memory_space=pltpu.VMEM)
     in_hbm = pl.BlockSpec(memory_space=pl.ANY)
     weights = attn_master.size + ffin_master.size + down_master.size
-    block_out, grad_tokens, owned_attn, owned_in, owned_down, owned_small, squares = pl.pallas_call(
+    block_out, grad_tokens, owned, owned_small, squares = pl.pallas_call(
         functools.partial(layer_kernel, (ny, nz, nx, per, ff_groups)),
         out_shape=[
             jax.ShapeDtypeStruct(square, bf16),
             jax.ShapeDtypeStruct(square, f32),
-            jax.ShapeDtypeStruct(attn_master.shape, f32),
-            jax.ShapeDtypeStruct(ffin_master.shape, f32),
-            jax.ShapeDtypeStruct(down_master.shape, f32),
+            jax.ShapeDtypeStruct((tiles, rows, TILE), f32),
             jax.ShapeDtypeStruct((1, 128), f32),
             jax.ShapeDtypeStruct((8, 128), f32),
         ],
         in_specs=[pl.BlockSpec(memory_space=pltpu.SMEM), in_vmem, in_vmem] + [in_hbm] * 5,
-        out_specs=[in_vmem] * 7,
+        out_specs=[in_hbm] + [in_vmem] * 4,
         scratch_shapes=scratch,
         compiler_params=pltpu.CompilerParams(
             collective_id=0, has_side_effects=True, vmem_limit_bytes=VMEM_BYTES
@@ -1332,44 +1841,73 @@
         ffin_master,
         down_master,
     )
-    grad_norm = jnp.sqrt(squares[0, 0])
-    clip_scale = clip_max / jnp.maximum(grad_norm, clip_max)
-    attn_new = adamw_update(
-        attn_master, attn_first, attn_second, owned_attn * clip_scale, matrix_rate, decay_rate
-    )
-    ffin_new = adamw_update(
-        ffin_master, ffin_first, ffin_second, owned_in * clip_scale, matrix_rate, decay_rate
-    )
-    down_new = adamw_update(
-        down_master, down_first, down_second, owned_down * clip_scale, matrix_rate, decay_rate
-    )
-    small_new = adamw_update(
-        small_master, small_first, small_second, owned_small[0, :per] * clip_scale, small_rate, 0.0
-    )
-    return (
+    like = [
+        jax.ShapeDtypeStruct((1, 1), f32),
+        *[jax.ShapeDtypeStruct((1, per), f32)] * 3,
+        jax.ShapeDtypeStruct(square, bf16),
+        jax.ShapeDtypeStruct(square, f32),
+        jax.ShapeDtypeStruct(attn_master.shape, f32),
+        jax.ShapeDtypeStruct(attn_master.shape, f32),
+        jax.ShapeDtypeStruct((3,) + attn_master.shape[1:], f32),
+        jax.ShapeDtypeStruct(attn_master.shape[1:], f32),
+        *[jax.ShapeDtypeStruct(ffin_master.shape, f32)] * 3,
+        *[jax.ShapeDtypeStruct(down_master.shape, f32)] * 3,
+    ]
+    results = pl.pallas_call(
+        functools.partial(update_kernel, (ff_groups,)),
+        out_shape=like,
+        in_specs=[in_vmem] * 5 + [in_hbm] * 12,
+        out_specs=[in_vmem] * 4 + [in_hbm] * 12,
+        scratch_shapes=[
+            vmem((tiles, rows, TILE), f32),
+            vmem((3,) + attn_master.shape, f32),
+            vmem((3,) + ffin_master.shape, f32),
+            vmem((3,) + down_master.shape, f32),
+            vmem(square, bf16),
+            vmem(square, f32),
+            dma((11,)),
+            dma((10,)),
+            dma((4,)),
+        ],
+        compiler_params=pltpu.CompilerParams(vmem_limit_bytes=VMEM_BYTES),
+        cost_estimate=pl.CostEstimate(
+            flops=20 * weights, bytes_accessed=28 * weights, transcendentals=2 * weights
+        ),
+    )(
+        squares,
+        owned_small,
+        small_master.reshape(1, per),
+        small_first.reshape(1, per),
+        small_second.reshape(1, per),
+        owned,
         block_out,
         grad_tokens,
-        grad_norm,
-        attn_new[0],
-        attn_new[1],
-        attn_new[2][1:],
-        attn_new[2][0],
-        ffin_new[0],
-        ffin_new[1],
-        ffin_new[2],
-        down_new[0],
-        down_new[1],
-        down_new[2],
-        small_new[0],
-        small_new[1],
-        small_new[2],
+        attn_master,
+        attn_first,
+        attn_second,
+        ffin_master,
+        ffin_first,
+        ffin_second,
+        down_master,
+        down_first,
+        down_second,
+    )
+    norm, small_new, small_one, small_two = results[:4]
+    return (
+        results[4],
+        results[5],
+        norm.reshape(()),
+        *results[6:],
+        small_new.reshape(per),
+        small_one.reshape(per),
+        small_two.reshape(per),
     )
 
 
 def choose(mesh, width):
     n_dp, n_fsdp = mesh.shape["dp"], mesh.shape["fsdp"]
     rows = width // (n_dp * n_fsdp)
-    if n_dp == 4 and n_fsdp % 2 == 0 and rows % (2 * HALF) == 0:
+    if n_dp == 4 and n_fsdp == 2 * LINE and rows % (2 * HALF) == 0:
         return functools.partial(fused_on_device, ny=n_dp // 2, nz=n_fsdp // 2, nx=2)
     return on_device
 

time: 289 us -> 247 us (0.85)
  Pallas kernels: 274 us -> 245 us
  other arithmetic: 6.32 us -> 0 us
  local copies, waits for them, and re-layouts: 6.28 us -> 1.3 us
    pallas_call x1, Pallas kernels: 274 us -> 237 us  [fused_on_device(): pl.pallas_call(functools.partial(layer_kernel, (ny, nz, nx, per, ff_group...]
    pallas_call x0 -> x1, Pallas kernels: none -> 7.63 us  [fused_on_device(): pl.pallas_call(functools.partial(update_kernel, (ff_groups,)), out_shape=...]
    sub x4 -> x0, other arithmetic: 6.32 us -> none  [adamw_update(): master - step_rate * (first_hat / (jnp.sqrt(second_hat) + adam_eps) + wei...]
where the time goes in v2:
time: 247 us
  Pallas kernels  245 us (99%)
    pallas_call x1, Pallas kernels, fused_on_device(): pl.pallas_call(functools.partial(layer_kernel, (ny, nz, nx, per, ff_group...  237 us
    pallas_call x1, Pallas kernels, fused_on_device(): pl.pallas_call(functools.partial(update_kernel, (ff_groups,)), out_shape=...  7.63 us

profile of v2, /device:TPU:0, one launch (start us, length us, event | category | flops | bytes accessed | tf_op | source)
XLA Modules:
  0.0 247.2 jit_solution(9079863814357506846)
XLA Ops:
  0.6 1.3 copy.32.page_ref
  1.9 237.4 %shard_map.279 = (bf16[512,1024]{1,0:T(8,128)(2,1)}, f32[512,1024]{1,0:T(8,128)}, f32[49,32,256]{2,1,0:T(8,128)}, f32[1,128]{1,0:T(1,128)}, f32[8,128]{1,0:T(8,128)}) custom-call(s32[2,1]{1,0:T(2,128)} %copy.32.page_ref, s32[2,512]{1,0:T(2,128)} %pos_ref.1, f32[1,112]{1,0:T(1,128)} %bitcast.7, bf16[512,1024]{1,0:T(8,128)(2,1)} %tok_hbm.1, ...), custom_call_target="tpu_custom_call" | custom-call | flops 39460012032 | bytes 9633792 | tf_op jit(solution)/shard_map/pallas_call | solution.py:1814
  239.4 7.6 %shard_map.280 = (f32[1,1]{1,0:T(1,128)}, f32[1,112]{1,0:T(1,128)}, f32[1,112]{1,0:T(1,128)}, f32[1,112]{1,0:T(1,128)}, bf16[512,1024]{1,0:T(8,128)(2,1)}, /*ind...) custom-call(f32[8,128]{1,0:T(8,128)} %get-tuple-element.37.total_ref, ...), custom_call_target="tpu_custom_call" | custom-call | flops 8028160 | bytes 11239424 | tf_op jit(solution)/shard_map/pallas_call | solution.py:1856

commit v3 on v2

--- a/solution.py
+++ b/solution.py
@@ -309,16 +309,21 @@
 HALF = 16
 SLOTS = 4
 VMEM_BYTES = 63 * 2**20
-Z_SLOTS = 10
+Z_SLOTS = 12
 AHEAD = 3
 LATE_GROUPS = 3
 SUM_LAG = 5
 Z_FIRST_SUMS = (1, 5, 9)
 LAGS = (1, 2, 3, 5, 7)
-LINE_LAG = 2
+LINE_LAG = 3
 D_SLOTS = 4
 VMEM_BYTES = 63 * 2**20
 FIRST_AHEAD = 0
+DIRECT = 3
+SKIP = 1000
+AG_LAGS = (1, 2, 3)
+LATE_TICK = 10
+LATE_STEP = 2
 LINE = 4
 QKV_GROUPS = 4
 OUT_GROUPS = 2
@@ -360,8 +365,8 @@
     ffin_hbm,
     down_hbm,
     out_hbm,
-    gtok_ref,
-    own,
+    gtok_hbm,
+    own_hbm,
     osmall_ref,
     norm_ref,
     w,
@@ -372,6 +377,8 @@
     rbz,
     rbd,
     rbe,
+    own,
+    mix,
     smb,
     sgr,
     sgz,
@@ -444,7 +451,9 @@
     inward = jnp.where(z < 2, 1, LINE - 2)
     far_end = LINE - 1 - edge
     dev_up, dev_down = device(y, c, jnp.minimum(z + 1, LINE - 1), x), device(y, c, jnp.maximum(z - 1, 0), x)
-    dev_across, dev_edge, dev_inward = (device(y, c, at, x) for at in (across, edge, inward))
+    dev_across, dev_edge, dev_inward, dev_far = (
+        device(y, c, at, x) for at in (across, edge, inward, far_end)
+    )
 
     def to_sides(send_up, send_down):
         pl.when(z < LINE - 1)(send_up)
@@ -601,16 +610,14 @@
             remote(landed, landed, s.at[0, b], r.at[0, b], dev_edge).start()
 
     def late_step(t, fn):
-        ticks = 3 * LATE_GROUPS * 3 // 2
         if isinstance(t, int):
-            if 1 <= t <= ticks and t % 3:
-                fn(t - 1 - t // 3)
+            if 1 <= t <= 3 * LATE_GROUPS:
+                fn(t - 1)
         else:
-            inside = jnp.logical_and(jnp.logical_and(t >= 1, t <= ticks), lax.rem(t, 3) != 0)
-
-            @pl.when(inside)
+
+            @pl.when(jnp.logical_and(t >= 1, t <= 3 * LATE_GROUPS))
             def _():
-                fn(t - 1 - t // 3)
+                fn(t - 1)
 
     def late4(g):
         def go(t0, count, g):
@@ -735,16 +742,34 @@
         def _():
             remote(one, one, s, r, sib).wait_send()
 
-    def ag_tick(t):
+    def ag_front(t):
         ag1(t + AHEAD)
         ag1_relay(t + FIRST_AHEAD + 1)
         ag2(t + FIRST_AHEAD)
         late_step(t, late_line)
-        ag3(t - 1)
+        ag3(t - AG_LAGS[0])
+
+    def ag_back(t):
         late_step(t - 3, late_relay)
-        ag4(t - 2)
-        late4(t - 2)
-        ag5(t - 3)
+        ag4(t - AG_LAGS[1])
+        late4(late_start + t - LATE_TICK)
+        ag5(jnp.where(t - AG_LAGS[2] < late_start, t - AG_LAGS[2], -1) if not isinstance(t, int) else (t - AG_LAGS[2] if t - AG_LAGS[2] < late_start else -1))
+
+    early_ff = ff_groups - LATE_GROUPS
+
+    def ff_step(s):
+        over = s - LATE_STEP
+        if isinstance(s, int):
+            if over < 0 or over >= 2 * LATE_GROUPS:
+                before = s if over < 0 else s - LATE_GROUPS
+                return before, False, before
+            late = over % 2 == 0
+            before = LATE_STEP + over // 2
+            return (early_ff + over // 2 if late else before), late, before
+        inside = jnp.logical_and(over >= 0, over < 2 * LATE_GROUPS)
+        late = jnp.logical_and(inside, lax.rem(over + 2 * LATE_GROUPS, 2) == 0)
+        before = jnp.where(over < 0, s, jnp.where(inside, LATE_STEP + over // 2, s - LATE_GROUPS))
+        return jnp.where(late, early_ff + over // 2, before), late, before
 
     def rs_group(n):
         if isinstance(n, int):
@@ -752,12 +777,12 @@
                 return -1
             tail = n - ff_groups
             if tail < 0:
-                return QKV_GROUPS + OUT_GROUPS + n
+                return QKV_GROUPS + OUT_GROUPS + ff_step(n)[0]
             return QKV_GROUPS + tail if tail < OUT_GROUPS else tail - OUT_GROUPS
         tail = n - ff_groups
         g = jnp.where(
             tail < 0,
-            QKV_GROUPS + OUT_GROUPS + n,
+            QKV_GROUPS + OUT_GROUPS + ff_step(n)[0],
             jnp.where(tail < OUT_GROUPS, QKV_GROUPS + tail, tail - OUT_GROUPS),
         )
         return jnp.where(jnp.logical_or(n < 0, n >= groups), -1, g)
@@ -858,6 +883,20 @@
     def dev_at(at):
         return jnp.clip(at, 0, LINE - 1)
 
+    def line_direct(part, landed, s, r):
+        to_sides(
+            lambda: remote(part(dev_at(z + 1)), landed(0), s(5), r(5), dev_up).start(),
+            lambda: remote(part(dev_at(z - 1)), landed(1), s(6), r(6), dev_down).start(),
+        )
+        remote(part(across), landed(2), s(7), r(7), dev_across).start()
+
+        @pl.when(jnp.logical_not(inner))
+        def _():
+            remote(part(far_end), landed(3), s(8), r(8), dev_far).start()
+
+    def is_direct(n):
+        return isinstance(n, int) and n >= groups - DIRECT
+
     def line_merge(part, landed, s, r, add):
         @pl.when(inner)
         def _():
@@ -886,6 +925,9 @@
         pl.when(jnp.logical_not(inner))(lambda: remote(part, part, s(8), r(8), sib).wait_send())
 
     def rs_merge(n):
+        if is_direct(n):
+            return
+
         def go(t0, count, slots, s, r):
             t = pl.ds(t0, count)
 
@@ -976,7 +1018,7 @@
                         + re[slot, 0, i, zz].astype(f32)
                         + re[slot, 1, i, zz].astype(f32)
                     ).astype(bf16)
-            line_sends(
+            (line_direct if is_direct(n) else line_sends)(
                 lambda at: w.at[t, y, c, at, x], lambda kind: rf.at[slots[1], kind, pl.ds(0, count)], s, r
             )
 
@@ -1007,6 +1049,13 @@
             line_wait(
                 lambda at: w.at[t, y, c, at, x], lambda kind: rf.at[slots[1], kind, pl.ds(0, count)], s, r, add
             )
+            if is_direct(n):
+
+                @pl.when(jnp.logical_not(inner))
+                def _():
+                    landed = rf.at[slots[1], 3, pl.ds(0, count)]
+                    remote(w.at[t, y, c, z, x], landed, s(8), r(8), dev_far).wait_recv()
+                    add(3)
 
         on_sum(n, go, False)
 
@@ -1048,12 +1097,14 @@
 
         on_sum(n, go_line, True)
 
-    def rs_tick(n):
+    def rs_front(n):
         rs0(n)
         rs1(n - LAGS[0])
         for i in range(3):
             rs1_line(n - LAGS[0] - i, i)
         rs2(n - LAGS[1])
+
+    def rs_back(n):
         rs3(n - LAGS[2])
         for i in range(3):
             rs_line_merge(n - LAGS[0] - LINE_LAG - i, i)
@@ -1062,6 +1113,10 @@
         rs2_line(n - LAGS[0] - 2 * LINE_LAG - 2)
         rs3_line(n - LAGS[0] - 2 * LINE_LAG - 3)
         rs4_line(n - LAGS[0] - 2 * LINE_LAG - 4)
+
+    def rs_tick(n):
+        rs_front(n)
+        rs_back(n)
 
     def cast_wait(copy):
         copy.wait_send()
@@ -1085,21 +1140,20 @@
     smb[near, z, 0:1, 0:per] = small_ref[...].astype(bf16).astype(f32)
     load_wait(0)
     pl.semaphore_wait(barrier, len(cube) + nz - 1)
+    ag1(0)
     sm_start(0)
-    ag1(0)
     for g in range(1, AHEAD):
         load_wait(g)
         ag1(g)
     for g in range(late_start, groups):
         load_wait(g)
         late1(g)
-    for g in range(AHEAD, late_start):
-        load_wait(g)
+    load_wait(AHEAD)
 
     lane = iota((tok_count, 128), 1)
     row = iota((tok_count, 128), 0)
-    first_len = page_ref[0, 0]
-    both_len = page_ref[0, 0] + page_ref[1, 0]
+    first_len = page_ref[:, 0:1]
+    both_len = first_len + page_ref[:, 1:2]
 
     def pos_rows(k):
         line = pos_ref[k : k + 1, :].astype(f32)
@@ -1116,15 +1170,18 @@
     k2[...] = jnp.where(lane < 64, hot_y, jnp.where(lane < 67, barred, 0.0)).astype(bf16)
     hxt[...] = hot_x.T[0:64].astype(bf16)
     hyt[...] = hot_y.T[0:64].astype(bf16)
-    sm_wait(0)
-    sm_start(1)
     for g in range(FIRST_AHEAD + 1):
         ag1_relay(g)
         if g < FIRST_AHEAD:
             ag2(g)
-    ag_tick(0)
+    ag_front(0)
+    ag_back(0)
+    sm_wait(0)
+    sm_start(1)
     for g in range(late_start, groups):
         late2(g)
+    for g in range(AHEAD + 1, late_start):
+        load_wait(g)
     cot_copy.wait()
 
     def mask_out(i, carry):
@@ -1138,7 +1195,8 @@
     lax.fori_loop(0, tok_count // 128, mask_out, 0)
     for g in range(late_start, groups):
         late3(g)
-    ag_tick(1)
+    ag_front(1)
+    ag_back(1)
     sm_wait(1)
 
     devs = [(a, b, d, e) for a in range(ny) for b in range(2) for d in range(nz) for e in range(nx)]
@@ -1212,7 +1270,10 @@
         return carry
 
     lax.fori_loop(0, tok_count // 128, norm_one, 0)
-    ag_tick(2)
+    for t in range(2, AG_LAGS[2]):
+        ag_front(t)
+        ag_back(t)
+    ag_front(AG_LAGS[2])
 
     def tile_of(t):
         return w[t].reshape(width, TILE)
@@ -1274,25 +1335,23 @@
             dest[2 * j + 1] = result[:, 128:256]
 
     def forward_heads(j, carry):
-        ag_tick(j + 3)
+        ag_back(j + AG_LAGS[2])
         project(j)
-
-        def one(i, inner):
-            forward_pair(2 * j + i)
-            return inner
-
-        lax.fori_loop(0, 2, one, 0)
+        forward_pair(2 * j)
+        ag_front(j + AG_LAGS[2] + 1)
+        forward_pair(2 * j + 1)
         return carry
 
     lax.fori_loop(0, QKV_GROUPS, forward_heads, 0)
-    ag_tick(7)
-    ag_tick(8)
+    tick = AG_LAGS[2] + QKV_GROUPS
+    for i in range(OUT_GROUPS):
+        ag_back(tick)
+        tick += 1
+        ag_front(tick)
 
     for e in range(4):
         cols = pl.ds(e * TILE, TILE)
         res[:, cols] = tok[:, cols].astype(f32) + dot(ctx[...], tile_of(OUT_START + e))
-
-    mix = gtok_ref
 
     def norm_two(i, carry):
         at = pl.ds(pl.multiple_of(i * 128, 128), 128)
@@ -1309,8 +1368,17 @@
 
     root = float(np.sqrt(2.0 / np.pi))
 
-    def feed(f, carry):
-        ag_tick(f + 9)
+    def feed(step, carry):
+        f, late, before = ff_step(step)
+
+        @pl.when(late)
+        def _():
+            ag5(jnp.where(late, QKV_GROUPS + OUT_GROUPS + f, -1))
+
+        @pl.when(jnp.logical_not(late))
+        def _():
+            ag_back(before + tick)
+
         t0 = FF_START + 3 * f
         gate_w, up_w, down_w = tile_of(t0), tile_of(t0 + 1), tile_of(t0 + 2)
         gate = dot(n2[...], gate_w)
@@ -1322,6 +1390,11 @@
         active = gate * half
         slope_of = half + 0.5 * gate * (1.0 - turn * turn) * (root * (1.0 + 3 * 0.044715 * square))
         hidden = (active * up).astype(bf16)
+
+        @pl.when(jnp.logical_not(late))
+        def _():
+            ag_front(before + tick + 1)
+
         grad_gate = (grad_hidden * up * slope_of).astype(bf16)
         grad_up = (grad_hidden * active).astype(bf16)
         mix[...] += dot_nt(hidden, down_w)
@@ -1331,7 +1404,7 @@
         w[t0] = dot(n2t[...], grad_gate).astype(bf16).reshape(shape)
         w[t0 + 1] = dot(n2t[...], grad_up).astype(bf16).reshape(shape)
         w[t0 + 2] = dot(goutt[...], hidden).astype(bf16).reshape(shape)
-        rs_tick(f - SUM_LAG)
+        rs_tick(step - SUM_LAG)
         return carry
 
     lax.fori_loop(0, ff_groups, feed, 0)
@@ -1376,7 +1449,9 @@
             w[OUT_START + e] = (
                 dot(ctxt[...], attended[:, pl.ds(e * TILE, TILE)]).astype(bf16).reshape(shape)
             )
-        rs_tick(done)
+        rs_front(done)
+        if i < OUT_GROUPS - 1:
+            rs_back(done)
         done += 1
 
     flip = (sq_row + sq_lane == 127).astype(f32).astype(bf16)
@@ -1389,7 +1464,7 @@
         rest = (value - high.astype(f32)).astype(bf16)
         return dot(matrix, high) + dot(matrix, rest)
 
-    def backward_pair(p, local):
+    def backward_pair(p, local, between):
         at = pl.ds(pl.multiple_of(p * 128, 128), 128)
         k_turned = kp[p].astype(f32).T.astype(bf16)
         grad_rows = gctx[:, at]
@@ -1426,6 +1501,8 @@
             dk_parts.append(dk_e)
             rolled = pltpu.roll(split_left(flip, acc[...]), 0, 1, stride=1, stride_axis=0)
             gv[h, 0:1, :] = jnp.sum(rolled, axis=0, keepdims=True)
+            if e == 0:
+                between()
         low = half_lane
         cols = pl.ds(local * 128, 128)
         dq[:, cols] = jnp.concatenate(dq_parts, axis=0).T.astype(bf16)
@@ -1438,10 +1515,16 @@
             dest[2 * p, 0:1, :] = jnp.sum(rolled[0:64], axis=0, keepdims=True)
             dest[2 * p + 1, 0:1, :] = jnp.sum(rolled[64:128], axis=0, keepdims=True)
 
+    first_head = ff_groups + OUT_GROUPS
+
+    def end_tick(j):
+        return jnp.minimum(done + 2 * j + 1, first_head + j)
+
     def backward_heads(j, carry):
-        backward_pair(2 * j, 0)
-        rs_tick(done + 2 * j)
-        backward_pair(2 * j + 1, 1)
+        middle = jnp.where(j <= first_head - 1 - done, done + 2 * j, -SKIP)
+        backward_pair(2 * j, 0, lambda: rs_back(end_tick(j - 1)))
+        rs_front(middle)
+        backward_pair(2 * j + 1, 1, lambda: rs_back(middle))
         gn[...] += (
             dot_nt(dq[...], tile_of(3 * j))
             + dot_nt(dk[...], tile_of(3 * j + 1))
@@ -1450,11 +1533,12 @@
         ag_sent(j)
         for i, part in enumerate((dq, dk, dv)):
             w[3 * j + i] = dot(n1t[...], part[...]).astype(bf16).reshape(shape)
-        rs_tick(done + 2 * j + 1)
+        rs_front(end_tick(j))
         return carry
 
     lax.fori_loop(0, QKV_GROUPS, backward_heads, 0)
-    done += 2 * QKV_GROUPS
+    done = min(done + 2 * QKV_GROUPS, groups)
+    rs_back(done - 1)
     rs_tick(done)
 
     def norm_one_back(i, carry):
@@ -1465,12 +1549,14 @@
         gsum[0] += jnp.sum((got * stream * scale).reshape(16, 8, width), axis=0)
         scaled = gains[0] * got
         inner = jnp.mean(scaled * stream, axis=-1, keepdims=True)
-        gtok_ref[at, :] = (
+        grad_res[at, :] = (
             grad_res[at, :] + scale * scaled - stream * (scale * scale * scale * inner)
         )
         return carry
 
     lax.fori_loop(0, tok_count // 128, norm_one_back, 0)
+    gtok_copy = pltpu.make_async_copy(grad_res, gtok_hbm, in_sem.at[1])
+    gtok_copy.start()
     rs_tick(done + 1)
 
     def unhot(bucket_col, count):
@@ -1556,6 +1642,8 @@
     mine = iota(small_total.shape, 0) == me
     osmall_ref[...] = jnp.sum(jnp.where(mine, small_total, 0.0), axis=0, keepdims=True)
 
+    own_copy = pltpu.make_async_copy(own, own_hbm, in_sem.at[2])
+    own_copy.start()
     squares = jnp.zeros((8, TILE), f32)
     for t in range(own.shape[0]):
         value = own[t]
@@ -1563,11 +1651,13 @@
     nbr[near] = squares[:, 0:128] + squares[:, 128:256]
     near_start(4, nbr)
     out_copy.wait()
+    gtok_copy.wait()
     for n in range(groups):
         rs_sent(n)
     near_sum(4, nbr, nbz)
     total = jnp.sum(line_sum(4, nbz)) + jnp.sum(small_total * small_total)
     norm_ref[...] = jnp.full((8, 128), 1.0, f32) * total
+    own_copy.wait()
 
 
 def update_kernel(
@@ -1641,11 +1731,9 @@
             pltpu.make_async_copy(src, state[i].at[k], in_sem.at[2 + 3 * i + k])
             for k, src in enumerate(sources[i])
         ]
-    for part in loads:
+    for part in (*loads, passing):
         for copy in part:
             copy.start()
-    for copy in passing:
-        copy.start()
     norm = jnp.sqrt(total_ref[0:1, 0:1])
     norm_out[...] = norm
     clip = clip_max / jnp.maximum(norm, clip_max)
@@ -1758,6 +1846,8 @@
         vmem((banks, 4, 3, ny, nx, rows, TILE), bf16),
         vmem((banks, 2, 3, HALF, TILE), bf16),
         vmem((banks, 2, 3, rows, TILE), bf16),
+        vmem((tiles, rows, TILE), f32),
+        vmem(square, f32),
         vmem((ny * 2 * nx, nz, 8, 128), f32),
         vmem((ny * 2 * nx, ny * 2 * nz * nx, 128), f32),
         vmem((nz, ny * 2 * nz * nx, 128), f32),
@@ -1796,7 +1886,7 @@
         vmem((2, 1, width), f32),
         vmem((2, 8, width), f32),
         dma((groups,)),
-        dma((2,)),
+        dma((3,)),
         dma((7, groups)),
         dma((7, groups)),
         dma((2, 3 * LATE_GROUPS)),
@@ -1820,8 +1910,8 @@
             jax.ShapeDtypeStruct((1, 128), f32),
             jax.ShapeDtypeStruct((8, 128), f32),
         ],
-        in_specs=[pl.BlockSpec(memory_space=pltpu.SMEM), in_vmem, in_vmem] + [in_hbm] * 5,
-        out_specs=[in_hbm] + [in_vmem] * 4,
+        in_specs=[in_vmem] * 3 + [in_hbm] * 5,
+        out_specs=[in_hbm] * 3 + [in_vmem] * 2,
         scratch_shapes=scratch,
         compiler_params=pltpu.CompilerParams(
             collective_id=0, has_side_effects=True, vmem_limit_bytes=VMEM_BYTES
@@ -1832,7 +1922,7 @@
             transcendentals=3 * tok_count * tok_count * HEADS,
         ),
     )(
-        page_lengths,
+        page_lengths.T,
         layout_pos,
         small_master.reshape(1, per),
         tokens,

time: 247 us -> 241 us (0.976)
  Pallas kernels: 245 us -> 240 us
    pallas_call x1, Pallas kernels: 237 us -> 232 us  [fused_on_device(): pl.pallas_call(functools.partial(layer_kernel, (ny, nz, nx, per, ff_group...]
where the time goes in v3:
time: 241 us; the launch traced here: 240 us
  Pallas kernels  240 us (100%)
    pallas_call x1, Pallas kernels, fused_on_device(): pl.pallas_call(functools.partial(layer_kernel, (ny, nz, nx, per, ff_group...  232 us
    pallas_call x1, Pallas kernels, fused_on_device(): pl.pallas_call(functools.partial(update_kernel, (ff_groups,)), out_shape=...  7.63 us

profile of v3, /device:TPU:0, one launch (start us, length us, event | category | flops | bytes accessed | tf_op | source)
XLA Modules:
  0.0 240.4 jit_solution(10953394756350137520)
XLA Ops:
  0.6 232.0 %shard_map.279 = (bf16[512,1024]{1,0:T(8,128)(2,1)}, f32[512,1024]{1,0:T(8,128)}, f32[49,32,256]{2,1,0:T(8,128)}, f32[1,128]{1,0:T(1,128)}, f32[8,128]{1,0:T(8,128)}) custom-call(s32[1,2]{1,0:T(1,128)} %bitcast.12, s32[2,512]{1,0:T(2,128)} %pos_ref.1, f32[1,112]{1,0:T(1,128)} %bitcast.8, bf16[512,1024]{1,0:T(8,128)(2,1)} %tok_hbm.1, ...), custom_call_target="tpu_custom_call" | custom-call | flops 39460012032 | bytes 9633792 | tf_op jit(solution)/shard_map/pallas_call | solution.py:1904
  232.6 7.6 %shard_map.280 = (f32[1,1]{1,0:T(1,128)}, f32[1,112]{1,0:T(1,128)}, f32[1,112]{1,0:T(1,128)}, f32[1,112]{1,0:T(1,128)}, bf16[512,1024]{1,0:T(8,128)(2,1)}, /*ind...) custom-call(f32[8,128]{1,0:T(8,128)} %get-tuple-element.37.total_ref, ...), custom_call_target="tpu_custom_call" | custom-call | flops 8028160 | bytes 11239424 | tf_op jit(solution)/shard_map/pallas_call | solution.py:1946

commit v4 on v3

--- a/solution.py
+++ b/solution.py
@@ -1319,9 +1319,9 @@
                 top = jnp.max(scores, axis=0, keepdims=True)
                 exponent = jnp.exp(scores - top)
                 total = jnp.sum(exponent, axis=0, keepdims=True)
-                probs = (exponent * (1.0 / total)).astype(bf16)
+                weights = exponent.astype(bf16)
                 lse[2 * p + e, 0:1, cols] = top + jnp.log(total)
-                parts.append(dot(v_turned[64 * e : 64 * (e + 1)], probs))
+                parts.append(dot(v_turned[64 * e : 64 * (e + 1)], weights) * (1.0 / total))
             pieces.append(jnp.concatenate(parts, axis=1))
         turned = jnp.concatenate(pieces, axis=0)
         at = pl.ds(pl.multiple_of(p * 128, 128), 128)
@@ -1635,19 +1635,26 @@
     near_start(2, sgr)
     rs_tick(done + 2)
     near_sum(2, sgr, sgz)
-    for n in range(done + 3, groups + LAGS[4]):
+    for n in range(done + 3, groups + LAGS[4] - 1):
         rs_tick(n)
     small_total = line_sum(2, sgz)
     me = ((y * 2 + c) * nz + z) * nx + x
     mine = iota(small_total.shape, 0) == me
     osmall_ref[...] = jnp.sum(jnp.where(mine, small_total, 0.0), axis=0, keepdims=True)
 
+    last = range(3 * (QKV_GROUPS - 1), 3 * QKV_GROUPS)
+
+    def add_squares(squares, tiles):
+        for t in tiles:
+            value = own[t]
+            squares = squares + jnp.sum((value * value).reshape(rows // 8, 8, TILE), axis=0)
+        return squares
+
+    squares = add_squares(jnp.zeros((8, TILE), f32), [t for t in range(own.shape[0]) if t not in last])
+    rs_tick(groups + LAGS[4] - 1)
     own_copy = pltpu.make_async_copy(own, own_hbm, in_sem.at[2])
     own_copy.start()
-    squares = jnp.zeros((8, TILE), f32)
-    for t in range(own.shape[0]):
-        value = own[t]
-        squares = squares + jnp.sum((value * value).reshape(rows // 8, 8, TILE), axis=0)
+    squares = add_squares(squares, last)
     nbr[near] = squares[:, 0:128] + squares[:, 128:256]
     near_start(4, nbr)
     out_copy.wait()

time: 241 us -> 241 us (level)
  no operation moved by 1% of the time
where the time goes in v4:
time: 241 us; the launch traced here: 240 us
  Pallas kernels  239 us (99%)
    pallas_call x1, Pallas kernels, fused_on_device(): pl.pallas_call(functools.partial(layer_kernel, (ny, nz, nx, per, ff_group...  232 us
    pallas_call x1, Pallas kernels, fused_on_device(): pl.pallas_call(functools.partial(update_kernel, (ff_groups,)), out_shape=...  7.63 us

profile of v4, /device:TPU:0, one launch (start us, length us, event | category | flops | bytes accessed | tf_op | source)
XLA Modules:
  0.0 240.3 jit_solution(8562793291549483315)
XLA Ops:
  0.6 231.8 %shard_map.279 = (bf16[512,1024]{1,0:T(8,128)(2,1)}, f32[512,1024]{1,0:T(8,128)}, f32[49,32,256]{2,1,0:T(8,128)}, f32[1,128]{1,0:T(1,128)}, f32[8,128]{1,0:T(8,128)}) custom-call(s32[1,2]{1,0:T(1,128)} %bitcast.12, s32[2,512]{1,0:T(2,128)} %pos_ref.1, f32[1,112]{1,0:T(1,128)} %bitcast.8, bf16[512,1024]{1,0:T(8,128)(2,1)} %tok_hbm.1, ...), custom_call_target="tpu_custom_call" | custom-call | flops 39460012032 | bytes 9633792 | tf_op jit(solution)/shard_map/pallas_call | solution.py:1911
  232.5 7.6 %shard_map.280 = (f32[1,1]{1,0:T(1,128)}, f32[1,112]{1,0:T(1,128)}, f32[1,112]{1,0:T(1,128)}, f32[1,112]{1,0:T(1,128)}, bf16[512,1024]{1,0:T(8,128)(2,1)}, /*ind...) custom-call(f32[8,128]{1,0:T(8,128)} %get-tuple-element.37.total_ref, ...), custom_call_target="tpu_custom_call" | custom-call | flops 8028160 | bytes 11239424 | tf_op jit(solution)/shard_map/pallas_call | solution.py:1953
